TPU v7x, 512 devices: a whole 4x8x8 slice. The times are simulated.
512 devices in a mesh: chan: 16 (over y, core), blk: 32 (over z, x).
Axes of the slice: x: 4, y: 8, z: 8, core: 2. Of those that a mesh axis runs over, the one named last changes fastest.
Arguments:
- comp_alms: float32 [3, 4, 32, 4096], P(None, None, 'blk', 'chan'), may hold values from -6 to 6
- legendre: bfloat16 [2, 32, 4096, 128], P(None, 'blk'), may hold values from -0.09375 to 0.09375
- inv_noise: float32 [16, 2, 128, 8192], P('chan', None, 'blk'), may hold values from 0.5 to 5
- beam_window: float32 [16, 4096], replicated, may hold values from 0.1 to 1
- mixing: float32 [16, 3], replicated, may hold values from 0.2 to 1.5
- channel_of: int32 [16], replicated, may hold values from 0 to 15, each once
- m_orders: int32 [32], replicated, may hold values from 0 to 4095, as said below
- cycle_of: int32 [128], replicated, may hold values from 0 to 127, each once
- cycle_pixels: int32 [128], replicated, may hold values from 4 to 8192, as said below
Outputs:
- normal_product: float32 [3, 4, 32, 4096], P(None, None, 'blk', 'chan')
Inputs may be any that keep to these rules, and one draw needn't show every extreme that they name: `m_orders`: the orders are distinct. `cycle_pixels`: each entry is 4 * min(h, 2048, 8192 - h) for some cycle number h of 1 to 8191; at least one entry equals 8192.
All inputs are finite; a program needn't handle non-finite values.
Results may differ from a plain program's by a relative error of at most 0.0022.
Values may be sent and summed in bfloat16 or wider, within the bound.
No kernel may reach another device: no remote copies, remote signals or barrier semaphores. Data moves between devices by JAX's collectives and lax.ppermute only.
A program may use at most 128 MiB of HBM per device.

v0:
```python
import math

import jax
import jax.numpy as jnp
from jax import lax
from jax.sharding import Mesh
from jax.sharding import PartitionSpec as P

CHAN = ("chan_0", "chan_1")


def cut_along(x, dim, size):
    before, after = (x.shape[:dim], x.shape[dim + 1 :])
    return jnp.moveaxis(x.reshape(*before, size, -1, *after), dim, 0)


def joined_along(pieces, dim):
    pieces = jnp.moveaxis(pieces, 0, dim)
    shape = pieces.shape
    return pieces.reshape(*shape[:dim], shape[dim] * shape[dim + 1], *shape[dim + 2 :])


def moved_by_axis(pieces, axes, turns):
    shape = [lax.axis_size(a) for a in axes]
    pieces = pieces.reshape(*shape, *pieces.shape[1:])
    for k in turns:
        pieces = lax.all_to_all(pieces, axes[k], split_axis=k, concat_axis=k, tiled=True)
    return pieces.reshape(-1, *pieces.shape[len(axes) :])


def exchange_by_axis(x, axes, turns, split_dim, concat_dim):
    pieces = cut_along(x, split_dim, lax.axis_size(axes))
    return joined_along(moved_by_axis(pieces, axes, turns), concat_dim)


def phase_rows(orders, pix_count, cycle_width):
    columns = jnp.arange(cycle_width, dtype=jnp.int32)
    phase_steps = orders[:, None] * (2 * columns[None, :] + 1) % (2 * pix_count)
    angles = phase_steps.astype(jnp.float32) * (
        jnp.float32(math.pi) / pix_count.astype(jnp.float32)
    )
    return jnp.concatenate([jnp.cos(angles), jnp.sin(angles)], axis=0).astype(jnp.bfloat16)


def combine_forward(plus_sum, minus_sum):
    return jnp.stack(
        [
            plus_sum[:, 0] - minus_sum[:, 3],
            plus_sum[:, 1] + minus_sum[:, 2],
            plus_sum[:, 2] + minus_sum[:, 1],
            plus_sum[:, 3] - minus_sum[:, 0],
        ],
        axis=1,
    )


def twist_grads(cycle_grads):
    return jnp.stack(
        [-cycle_grads[:, 3], cycle_grads[:, 2], cycle_grads[:, 1], -cycle_grads[:, 0]], axis=1
    )


def cycle_work(coeffs, weights, orders, pix_count):
    slots = coeffs.shape[0]
    cycle_width = weights.shape[-1]
    phases = phase_rows(orders, pix_count, cycle_width)
    half_rows = phases.shape[0] // 2
    real_part = coeffs[:, 0::2]
    imag_part = coeffs[:, 1::2]
    stacked = jnp.concatenate([real_part, -imag_part], axis=2).reshape(2 * slots, 2 * half_rows)
    maps = jnp.dot(stacked, phases, preferred_element_type=jnp.float32)
    live_mask = jnp.arange(cycle_width, dtype=jnp.int32) < pix_count
    scaled = jnp.where(live_mask[None, None, :], weights, 0.0) / pix_count.astype(jnp.float32)
    weighted = (scaled.reshape(maps.shape) * maps).astype(jnp.bfloat16)
    returned = lax.dot_general(
        weighted, phases, (((1,), (1,)), ((), ())), preferred_element_type=jnp.float32
    )
    grad_real = returned[:, :half_rows].reshape(slots, 2, half_rows)
    grad_imag = (-returned[:, half_rows:]).reshape(slots, 2, half_rows)
    return (
        jnp.stack([grad_real, grad_imag], axis=2).reshape(slots, 4, half_rows).astype(jnp.bfloat16)
    )


def mix_components(mix_rows, components):
    accum = mix_rows[:, 0, None, None, None] * components[0][None]
    for comp_index in range(1, components.shape[0]):
        accum = accum + mix_rows[:, comp_index, None, None, None] * components[comp_index][None]
    return accum


def body(
    comp_alms,
    legendre,
    inv_noise,
    beam_window,
    mixing,
    channel_of,
    m_orders,
    cycle_of,
    cycle_pixels,
):
    chan_index = lax.axis_index(CHAN)
    blk_index = lax.axis_index("blk")
    order_dev = comp_alms.shape[2]
    shard_len = comp_alms.shape[3]
    length = legendre.shape[2]
    cycle_total = legendre.shape[3]
    chan_dev = inv_noise.shape[0]
    cycle_dev = inv_noise.shape[2]
    block_len = min(512, length)
    blocks = length // block_len
    own_orders = lax.dynamic_slice_in_dim(m_orders, blk_index * order_dev, order_dev)
    keep_mask = (jnp.arange(length, dtype=jnp.int32)[None, :] >= own_orders[:, None]).astype(
        jnp.float32
    )
    mix_all = jnp.take(mixing, channel_of, axis=0)
    beam_piece = jnp.take(
        lax.dynamic_slice_in_dim(beam_window, chan_index * shard_len, shard_len, 1),
        channel_of,
        axis=0,
    )
    degrees = chan_index * shard_len + jnp.arange(shard_len, dtype=jnp.int32)
    keep_piece = (degrees[None, :] >= own_orders[:, None]).astype(jnp.float32)
    mixed_alm = mix_components(mix_all, comp_alms)
    local_alm = (mixed_alm * beam_piece[:, None, None, :] * keep_piece[None, None]).astype(
        jnp.bfloat16
    )
    chan_alm = lax.all_to_all(local_alm, CHAN, split_axis=0, concat_axis=3, tiled=True)
    order = 0
    row_block = chan_alm[:, :, order, :].reshape(chan_dev * 4, length)
    first_block = own_orders[order] // block_len

    def add_block(index, running, row_block=row_block, order=order):
        plus_sum, minus_sum = running
        offset = index * block_len
        segment = lax.dynamic_slice_in_dim(row_block, offset, block_len, 1)
        tables = lax.dynamic_slice(legendre, (0, order, offset, 0), (2, 1, block_len, cycle_total))
        plus_sum = plus_sum + jnp.dot(segment, tables[0, 0], preferred_element_type=jnp.float32)
        minus_sum = minus_sum + jnp.dot(segment, tables[1, 0], preferred_element_type=jnp.float32)
        return (plus_sum, minus_sum)

    zeros_cycle = jnp.zeros((chan_dev * 4, cycle_total), jnp.float32)
    plus_sum, minus_sum = lax.fori_loop(first_block, blocks, add_block, (zeros_cycle, zeros_cycle))
    coeff_list = [
        combine_forward(
            plus_sum.reshape(chan_dev, 4, cycle_total), minus_sum.reshape(chan_dev, 4, cycle_total)
        )
    ]
    cycle_coeffs = jnp.stack(coeff_list, axis=2).astype(jnp.bfloat16)
    slot_coeffs = jnp.take(cycle_coeffs, cycle_of, axis=3)
    by_cycle = lax.all_to_all(slot_coeffs, "blk", split_axis=3, concat_axis=2, tiled=True)
    first_slot = blk_index * cycle_dev

    def per_cycle(index, collected):
        coeffs = lax.dynamic_index_in_dim(by_cycle, index, 3, keepdims=False)
        weights = lax.dynamic_index_in_dim(inv_noise, index, 2, keepdims=False)
        pix_count = cycle_pixels[cycle_of[first_slot + index]]
        result = cycle_work(coeffs, weights, m_orders, pix_count)
        return lax.dynamic_update_index_in_dim(collected, result, index, 3)

    slot_grads = lax.fori_loop(0, cycle_dev, per_cycle, jnp.zeros(by_cycle.shape, jnp.bfloat16))
    returned = lax.all_to_all(slot_grads, "blk", split_axis=2, concat_axis=3, tiled=True)
    inverse = (
        jnp.zeros((cycle_total,), jnp.int32)
        .at[cycle_of]
        .set(jnp.arange(cycle_total, dtype=jnp.int32))
    )
    cycle_grads = jnp.take(returned, inverse, axis=3)
    order = 0
    order_grads = cycle_grads[:, :, order, :]
    twisted = twist_grads(order_grads).reshape(chan_dev * 4, cycle_total)
    straight = order_grads.reshape(chan_dev * 4, cycle_total)
    first_block = own_orders[order] // block_len

    def add_degrees(index, accum, straight=straight, twisted=twisted, order=order):
        offset = index * block_len
        tables = lax.dynamic_slice(legendre, (0, order, offset, 0), (2, 1, block_len, cycle_total))
        segment = lax.dot_general(
            straight, tables[0, 0], (((1,), (1,)), ((), ())), preferred_element_type=jnp.float32
        )
        segment = segment + lax.dot_general(
            twisted, tables[1, 0], (((1,), (1,)), ((), ())), preferred_element_type=jnp.float32
        )
        return lax.dynamic_update_slice_in_dim(accum, segment, offset, 1)

    accum = lax.fori_loop(
        first_block, blocks, add_degrees, jnp.zeros((chan_dev * 4, length), jnp.float32)
    )
    grad_list = [accum.reshape(chan_dev, 4, length)]
    alm_grads = jnp.stack(grad_list, axis=2) * keep_mask[None, None]
    received = exchange_by_axis(alm_grads, CHAN, (1, 0), 3, 0)
    beamed = received * beam_piece[:, None, None, :]
    return jnp.einsum("kc,kpml->cpml", mix_all, beamed, precision=lax.Precision.HIGHEST)


def solution(mesh):
    split = Mesh(mesh.devices.reshape(8, 2, mesh.shape["blk"]), ("chan_0", "chan_1", "blk"))
    placed = (
        P(None, None, "blk", CHAN),
        P(None, "blk", None, None),
        P(CHAN, None, "blk", None),
        P(),
        P(),
        P(),
        P(),
        P(),
        P(),
    )
    return jax.shard_map(
        body, mesh=split, in_specs=placed, out_specs=P(None, None, "blk", CHAN), check_vma=False
    )
```

profile of v0, /device:TPU:1, one launch (start us, length us, event | category | flops | bytes accessed | tf_op | source)
XLA Modules:
  0.0 193.6 jit_solution(15667006930345607979)
XLA Ops:
  1.4 1.2 dynamic_slice.45
  7.0 10.1 %all-to-all-start = ((bf16[16,4,1,256]{3,1,2,0:T(4,128)(2,1)}), bf16[16,4,1,256]{3,1,2,0:T(4,128)(2,1)S(1)}, u32[]{:S(2)}, u32[]{:S(2)}) async-start(bf16[16,4,1,256]{3,1,2,0:T(4,128)(2,1)} %multiply_convert_fusion), calls=%async_computation | async-start | bytes 65536 | tf_op jit(solution)/shard_map/all_to_all | solution.py:129
  22.1 2.5 %all-to-all-done = bf16[16,4,1,256]{3,1,2,0:T(4,128)(2,1)S(1)} async-done(((bf16[16,4,1,256]{3,1,2,0:T(4,128)(2,1)}), bf16[16,4,1,256]{3,1,2,0:T(4,128)(2,1)S(1)}, u32[]{:S(2)}, u32[]{:S(2)}) %all-to-all-start) | async-done | bytes 32800 | tf_op jit(solution)/shard_map/all_to_all | solution.py:129
  24.6 12.5 %while.35 = (s32[]{:T(128)}, f32[4,128]{1,0:T(4,128)S(1)}, f32[4,128]{1,0:T(4,128)S(1)}, bf16[4,4096]{1,0:T(4,128)(2,1)S(1)}, bf16[2,1,4096,128]{3,2,1,0:T(8,128...) while((s32[]{:T(128)}, f32[4,128]{1,0:T(4,128)S(1)}, f32[4,128]{1,0:T(4,128)S(1)}, ...), condition=%wide.region_1.2_spmd, body=%wide.region_0.1_spmd.sunk | while | flops 1049607 | bytes 281247 | solution.py:144
  38.8 15.4 %all-to-all-start.1 = ((bf16[1,4,1,128]{1,2,0,3:T(2,128)(2,1)}), bf16[1,4,1,128]{1,2,0,3:T(2,128)(2,1)S(1)}, u32[]{:S(2)}, u32[]{:S(2)}) async-start(bf16[1,4,1,128]{1,2,0,3:T(2,128)(2,1)} %copy.68), calls=%async_computation.1 | async-start | bytes 131072 | tf_op jit(solution)/shard_map/all_to_all | solution.py:152
  55.0 8.1 %all-to-all-done.1 = bf16[1,4,1,128]{1,2,0,3:T(2,128)(2,1)S(1)} async-done(((bf16[1,4,1,128]{1,2,0,3:T(2,128)(2,1)}), bf16[1,4,1,128]{1,2,0,3:T(2,128)(2,1)S(1)}, u32[]{:S(2)}, u32[]{:S(2)}) %all-to-all-start.1) | async-done | bytes 1056 | tf_op jit(solution)/shard_map/all_to_all | solution.py:152
  63.2 85.0 %while.36 = (s32[]{:T(128)}, bf16[1,4,32,4]{2,1,3,0:T(4,128)(2,1)S(1)}, s32[]{:T(128)}, s32[128]{0:T(128)S(1)}, s32[128]{0:T(128)S(1)}, /*index=5*/f32[1,2,4,819...) while((s32[]{:T(128)}, ...), condition=%wide.region_3.5_spmd, body=%wide.region_2.4_spmd.sunk | while | flops 11625423 | bytes 2382145 | solution.py:162
  67.7 14.2 %cosine_convert_fusion.2 = (bf16[32,8192]{1,0:T(8,128)(2,1)S(1)}, bf16[32,8192]{1,0:T(8,128)(2,1)S(1)}) fusion(f32[]{:T(128)S(6)} %div.51, s32[]{:T(128)S(6)} %select_n.165, s32[8192]{0:T(1024)S(1)} %multiply_add_fusion.2, s32[32]{0:T(128)S(1)} %get-tuple-element.504, pred[]{:T(512)S(6)} %lt.143), kind=kLoop, calls=%fused_computation.23.clone.1 | loop fusion | flops 3145728 | bytes 1081481 | tf_op jit(solution)/shard_map/convert.5
  89.0 14.2 %cosine_convert_fusion.2 = (bf16[32,8192]{1,0:T(8,128)(2,1)S(1)}, bf16[32,8192]{1,0:T(8,128)(2,1)S(1)}) fusion(f32[]{:T(128)S(6)} %div.51, s32[]{:T(128)S(6)} %select_n.165, s32[8192]{0:T(1024)S(1)} %multiply_add_fusion.2, s32[32]{0:T(128)S(1)} %get-tuple-element.504, pred[]{:T(512)S(6)} %lt.143), kind=kLoop, calls=%fused_computation.23.clone.1 | loop fusion | flops 3145728 | bytes 1081481 | tf_op jit(solution)/shard_map/convert.5
  110.2 14.2 %cosine_convert_fusion.2 = (bf16[32,8192]{1,0:T(8,128)(2,1)S(1)}, bf16[32,8192]{1,0:T(8,128)(2,1)S(1)}) fusion(f32[]{:T(128)S(6)} %div.51, s32[]{:T(128)S(6)} %select_n.165, s32[8192]{0:T(1024)S(1)} %multiply_add_fusion.2, s32[32]{0:T(128)S(1)} %get-tuple-element.504, pred[]{:T(512)S(6)} %lt.143), kind=kLoop, calls=%fused_computation.23.clone.1 | loop fusion | flops 3145728 | bytes 1081481 | tf_op jit(solution)/shard_map/convert.5
  131.4 14.2 %cosine_convert_fusion.2 = (bf16[32,8192]{1,0:T(8,128)(2,1)S(1)}, bf16[32,8192]{1,0:T(8,128)(2,1)S(1)}) fusion(f32[]{:T(128)S(6)} %div.51, s32[]{:T(128)S(6)} %select_n.165, s32[8192]{0:T(1024)S(1)} %multiply_add_fusion.2, s32[32]{0:T(128)S(1)} %get-tuple-element.504, pred[]{:T(512)S(6)} %lt.143), kind=kLoop, calls=%fused_computation.23.clone.1 | loop fusion | flops 3145728 | bytes 1081481 | tf_op jit(solution)/shard_map/convert.5
  148.9 3.8 %all-to-all-start.2 = ((bf16[1,4,32,4]{1,3,0,2:T(4,128)(2,1)}), bf16[1,4,32,4]{1,3,0,2:T(4,128)(2,1)S(1)}, u32[]{:S(2)}, u32[]{:S(2)}) async-start(bf16[1,4,32,4]{1,3,0,2:T(4,128)(2,1)} %copy.72), calls=%async_computation.2 | async-start | bytes 65536 | tf_op jit(solution)/shard_map/all_to_all | solution.py:163
  152.8 8.6 %all-to-all-done.2 = bf16[1,4,32,4]{1,3,0,2:T(4,128)(2,1)S(1)} async-done(((bf16[1,4,32,4]{1,3,0,2:T(4,128)(2,1)}), bf16[1,4,32,4]{1,3,0,2:T(4,128)(2,1)S(1)}, u32[]{:S(2)}, u32[]{:S(2)}) %all-to-all-start.2) | async-done | bytes 1056 | tf_op jit(solution)/shard_map/all_to_all | solution.py:163
  162.2 12.7 %while.37 = (s32[]{:T(128)}, f32[4,4096]{1,0:T(4,128)S(1)}, bf16[2,1,4096,128]{3,2,1,0:T(8,128)(2,1)}, bf16[4,128]{1,0:T(4,128)(2,1)S(1)}, bf16[4,128]{1,0:T(4,1...) while((s32[]{:T(128)}, f32[4,4096]{1,0:T(4,128)S(1)}, ...), condition=%wide.region_6.8_spmd, body=%wide.region_5.7_spmd.sunk | while | flops 1050631 | bytes 290467 | solution.py:187
  163.3 1.1 fusion.67
  164.4 1.1 fusion.66
  165.4 1.1 fusion.67
  167.5 1.1 fusion.67
  169.7 1.1 fusion.67
  171.8 1.1 fusion.67
  172.8 1.1 fusion.66
  173.9 1.1 fusion.67
  175.0 6.4 %all_to_all.49 = f32[8,2,1,4,1,256]{5,0,3,4,2,1:T(8,128)S(1)} all-to-all(f32[8,2,1,4,1,256]{5,0,3,4,2,1:T(8,128)S(1)} %copy.75), channel_id=1, replica_groups=mesh['chan_0'=8,'chan_1'=2,'blk'=32] {'chan_1'}, dimensions={1} | all-to-all | bytes 131072 | tf_op jit(solution)/shard_map/all_to_all | solution.py:27
  181.5 11.2 %all_to_all.50 = f32[8,2,1,4,1,256]{5,1,3,4,2,0:T(2,128)S(1)} all-to-all(f32[8,2,1,4,1,256]{5,1,3,4,2,0:T(2,128)S(1)} %copy.76), channel_id=1, replica_groups=mesh['chan_0'=8,'chan_1'=2,'blk'=32] {'chan_0'}, dimensions={0} | all-to-all | bytes 131072 | tf_op jit(solution)/shard_map/all_to_all | solution.py:27
  (133 shorter events, 44.5 us)
Async XLA Ops:
  0.0 4.8 %copy-start = (f32[16,4096]{1,0:T(8,128)S(1)}, f32[16,4096]{1,0:T(8,128)}, u32[]{:S(2)}) copy-start(f32[16,4096]{1,0:T(8,128)} %param.20) | copy-start | bytes 786436
  0.0 63.2 %copy-start.1 = (s32[32]{0:T(128)S(1)}, s32[32]{0:T(128)}, u32[]{:S(2)}) copy-start(s32[32]{0:T(128)} %param.23) | copy-start | bytes 388
  0.0 63.2 %copy-start.2 = (s32[128]{0:T(128)S(1)}, s32[128]{0:T(128)}, u32[]{:S(2)}) copy-start(s32[128]{0:T(128)} %param.24) | copy-start | bytes 1540
  0.0 63.2 %copy-start.3 = (s32[128]{0:T(128)S(1)}, s32[128]{0:T(128)}, u32[]{:S(2)}) copy-start(s32[128]{0:T(128)} %param.25) | copy-start | bytes 1540
  7.0 17.6 %all-to-all-start = ((bf16[16,4,1,256]{3,1,2,0:T(4,128)(2,1)}), bf16[16,4,1,256]{3,1,2,0:T(4,128)(2,1)S(1)}, u32[]{:S(2)}, u32[]{:S(2)}) async-start(bf16[16,4,1,256]{3,1,2,0:T(4,128)(2,1)} %multiply_convert_fusion), calls=%async_computation | async-start | bytes 65536 | tf_op jit(solution)/shard_map/all_to_all | solution.py:129
  38.8 24.3 %all-to-all-start.1 = ((bf16[1,4,1,128]{1,2,0,3:T(2,128)(2,1)}), bf16[1,4,1,128]{1,2,0,3:T(2,128)(2,1)S(1)}, u32[]{:S(2)}, u32[]{:S(2)}) async-start(bf16[1,4,1,128]{1,2,0,3:T(2,128)(2,1)} %copy.68), calls=%async_computation.1 | async-start | bytes 131072 | tf_op jit(solution)/shard_map/all_to_all | solution.py:152
  148.9 12.4 %all-to-all-start.2 = ((bf16[1,4,32,4]{1,3,0,2:T(4,128)(2,1)}), bf16[1,4,32,4]{1,3,0,2:T(4,128)(2,1)S(1)}, u32[]{:S(2)}, u32[]{:S(2)}) async-start(bf16[1,4,32,4]{1,3,0,2:T(4,128)(2,1)} %copy.72), calls=%async_computation.2 | async-start | bytes 65536 | tf_op jit(solution)/shard_map/all_to_all | solution.py:163
where the time goes:
time: 196 us; the launch traced here: 194 us
  other arithmetic  65.3 us (33%)
  starting transfers between devices  29.4 us (15%)
  matrix products  27.7 us (14%)
  waiting for transfers between devices  19.3 us (10%)
  local copies, waits for them, and re-layouts  18.2 us (9%)
  blocking collectives  17.6 us (9%)
  loops' own time  13.3 us (7%)
  between operations  2.85 us (1%)
    another operation x5, other arithmetic  57 us
    all_to_all x2, blocking collectives, moved_by_axis(): lax.all_to_all(pieces, axes[k], split_axis=k, concat_axis=k, tiled=True)  17.6 us
    all_to_all x1, starting transfers between devices, body(): lax.all_to_all(slot_coeffs, 'blk', split_axis=3, concat_axis=2, tiled=True)  15.4 us
    another operation x1, loops' own time, body(): lax.fori_loop(0, cycle_dev, per_cycle, jnp.zeros(by_cycle.shape, jnp.bflo...  13.2 us
    all_to_all x1, starting transfers between devices, body(): lax.all_to_all(local_alm, CHAN, split_axis=0, concat_axis=3, tiled=True)  10.1 us
    all_to_all x1, waiting for transfers between devices, body(): lax.all_to_all(slot_grads, 'blk', split_axis=2, concat_axis=3, tiled=True)  8.61 us
    all_to_all x1, waiting for transfers between devices, body(): lax.all_to_all(slot_coeffs, 'blk', split_axis=3, concat_axis=2, tiled=True)  8.15 us
    dot_general x6, matrix products, add_degrees(): lax.dot_general(twisted, tables[1, 0], (((1,), (1,)), ((), ())), preferre...  6.36 us
  transfers between devices with their start and end apart: 3, of which 3 were waited for; matrix products, arithmetic and copies ran while one was open for 2% of the time, Pallas kernels for 0%

commit v1 on v0

v1 whole, which is shorter than its diff:
```python
import functools

import jax
import jax.numpy as jnp
from jax import lax
from jax.experimental import pallas as pl
from jax.experimental.pallas import tpu as pltpu
from jax.sharding import PartitionSpec as P

F32 = jnp.float32
BF16 = jnp.bfloat16
LANES = 128
NT = (((1,), (1,)), ((), ()))
TN = (((0,), (0,)), ((), ()))
NN = (((1,), (0,)), ((), ()))
COS = (0.9999999887921183, -19.739204415555925, 64.93911321613162, -85.45006149635309,
       60.16698573653733, -25.965151588112157, 6.525190124026944)
SIN = (6.28318530240345, -41.341700371179485, 81.60512965170976, -76.70298335354587,
       42.02566158843437, -14.898837201069828, 3.2367039052082127)

SMEM = pl.BlockSpec(memory_space=pltpu.SMEM)
VMEM = pl.BlockSpec(memory_space=pltpu.VMEM)
ANY = pl.BlockSpec(memory_space=pl.ANY)


def nearest(x):
    return jnp.floor(x + 0.5)


def poly(z, terms):
    total = jnp.full_like(z, terms[-1])
    for term in terms[-2::-1]:
        total = total * z + term
    return total


def cos_turns(y):
    return poly(y * y, COS)


def sin_turns(y):
    return y * poly(y * y, SIN)


def turns_of(steps, period):
    inverse = 1.0 / period
    rest = steps - nearest(steps * inverse) * period
    return rest * inverse


def forward_kernel(
    chan_of, mixing, orders, comp, beam, legendre, out, beam_s, leg_s, alm_s, sems, *, chan, blk
):
    width = comp.shape[3]
    first = chan() * width
    copies = [
        pltpu.make_async_copy(beam.at[:, pl.ds(first, width)], beam_s, sems.at[0]),
        pltpu.make_async_copy(legendre.at[0, 0, pl.ds(first, width), :], leg_s.at[pl.ds(0, width)], sems.at[1]),
        pltpu.make_async_copy(legendre.at[1, 0, pl.ds(first, width), :], leg_s.at[pl.ds(width, width)], sems.at[2]),
    ]
    for copy in copies:
        copy.start()
    order = orders[blk()]
    degrees = first + lax.broadcasted_iota(jnp.int32, (1, width), 1)
    keep = jnp.where(degrees >= order, 1.0, 0.0)
    parts = [comp[c, :, 0, :] for c in range(comp.shape[0])]
    copies[0].wait()
    for k in range(out.shape[0]):
        channel = chan_of[k]
        mixed = mixing[channel, 0] * parts[0]
        for c in range(1, len(parts)):
            mixed = mixed + mixing[channel, c] * parts[c]
        alm = mixed * beam_s[pl.ds(channel, 1), :] * keep
        twisted = jnp.concatenate([-alm[3:4], alm[2:3], alm[1:2], -alm[0:1]], axis=0)
        alm_s[4 * k : 4 * k + 4, :width] = alm
        alm_s[4 * k : 4 * k + 4, width:] = twisted
    copies[1].wait()
    copies[2].wait()
    sums = lax.dot_general(alm_s[...].astype(BF16), leg_s[...], NN, preferred_element_type=F32)
    out[...] = sums.reshape(out.shape)


def cycle_kernel(cycle_of, cycle_pixels, orders, coeffs, noise, out, *, blk, slots):
    count = orders.shape[0]
    lane = lax.broadcasted_iota(jnp.int32, (8, LANES), 1)
    order_row = jnp.zeros((8, LANES), F32)
    for i in range(count):
        order_row = jnp.where(lane // 4 == i, orders[i].astype(F32), order_row)
    m = order_row[:1]
    odd8 = lane % 2 == 1
    odd = odd8[:1]
    is_q = (lane % 4 < 2)[:1]
    sign = jnp.where(odd, -1.0, 1.0)

    def swap(x):
        up = pltpu.roll(x, LANES - 1, 1)
        down = pltpu.roll(x, 1, 1)
        return jnp.where(odd8, down, up)

    first = blk() * slots
    cycles = [cycle_of[first + r] for r in range(slots)]
    row8 = lax.broadcasted_iota(jnp.int32, (8, LANES), 0)
    chosen8 = jnp.full((8, LANES), -1, jnp.int32)
    for r in range(slots):
        chosen8 = jnp.where(row8 == r, cycles[r], chosen8)
    pick = jnp.where(lane == chosen8, 1.0, 0.0).astype(BF16)
    table = coeffs[...].reshape(4 * count, LANES)
    x = lax.dot_general(pick, table, NT, preferred_element_type=F32)
    x_sign = x * jnp.where(odd8, -1.0, 1.0)
    x_swap = swap(x)

    half = noise.shape[0] // 2
    tall = half // slots
    steps_a = lax.broadcasted_iota(jnp.int32, (tall, LANES), 0).astype(F32) * m * 32.0
    steps_b = (2 * lax.broadcasted_iota(jnp.int32, (LANES, LANES), 0) + 1).astype(F32) * m
    quarter = jnp.where(odd, 0.25, 0.0)
    pixel = (
        lax.broadcasted_iota(jnp.int32, (tall, LANES), 0) * LANES
        + lax.broadcasted_iota(jnp.int32, (tall, LANES), 1)
    )
    grads = jnp.zeros((8, LANES), F32)
    for r in range(slots):
        pixels = cycle_pixels[cycles[r]]
        number = jnp.full((1, LANES), pixels, jnp.int32).astype(F32)
        inverse = 1.0 / number
        ya = turns_of(steps_a, number * 0.25)
        ya = ya - nearest(ya)
        cos_a = cos_turns(ya)
        sin_a = sin_turns(ya)
        yb = turns_of(steps_b, number * 2.0) - quarter
        yb = yb - nearest(yb)
        phases = cos_turns(yb).astype(BF16)
        left = x_sign[r : r + 1] * cos_a - x_swap[r : r + 1] * sin_a
        left = jnp.concatenate([jnp.where(is_q, left, 0.0), jnp.where(is_q, 0.0, left)], axis=0)
        maps = lax.dot_general(left.astype(BF16), phases, NT, preferred_element_type=F32)
        live = jnp.where(pixel < pixels, inverse, 0.0)
        weights = jnp.concatenate(
            [noise[pl.ds(r, tall, stride=slots), :] * live, noise[pl.ds(half + r, tall, stride=slots), :] * live],
            axis=0,
        )
        weighted = (weights * maps).astype(BF16)
        back = lax.dot_general(weighted, phases, NN, preferred_element_type=F32)
        back = jnp.where(is_q, back[:tall], back[tall:])
        total_cos = jnp.sum(cos_a * back, axis=0, keepdims=True)
        total_sin = jnp.sum(sin_a * back, axis=0, keepdims=True)
        grad = sign * total_cos - swap(jnp.broadcast_to(total_sin, (8, LANES)))[:1]
        grads = jnp.where(row8 == r, grad, grads)
    spread = lax.dot_general(grads.astype(BF16), pick, TN, preferred_element_type=F32)
    out[...] = spread.astype(BF16).reshape(out.shape)


def adjoint_kernel(
    chan_of, mixing, orders, grads, beam, legendre, out, beam_s, leg_s, sems, *, chan, blk
):
    width = out.shape[3]
    first = chan() * width
    copies = [
        pltpu.make_async_copy(beam.at[:, pl.ds(first, width)], beam_s, sems.at[0]),
        pltpu.make_async_copy(legendre.at[0, 0, pl.ds(first, width), :], leg_s.at[0], sems.at[1]),
        pltpu.make_async_copy(legendre.at[1, 0, pl.ds(first, width), :], leg_s.at[1], sems.at[2]),
    ]
    for copy in copies:
        copy.start()
    order = orders[blk()]
    degrees = first + lax.broadcasted_iota(jnp.int32, (1, width), 1)
    keep = jnp.where(degrees >= order, 1.0, 0.0)
    slots = grads.shape[0]
    straight = grads[...].astype(F32).reshape(slots * 4, LANES)
    row = lax.broadcasted_iota(jnp.int32, straight.shape, 0) % 4
    up = pltpu.roll(straight, straight.shape[0] - 1, 0)
    down = pltpu.roll(straight, 1, 0)
    up3 = pltpu.roll(straight, straight.shape[0] - 3, 0)
    down3 = pltpu.roll(straight, 3, 0)
    twisted = jnp.where(row == 0, -up3, jnp.where(row == 1, up, jnp.where(row == 2, down, -down3)))
    for copy in copies:
        copy.wait()
    sums = lax.dot_general(straight.astype(BF16), leg_s[0], NT, preferred_element_type=F32)
    sums = sums + lax.dot_general(twisted.astype(BF16), leg_s[1], NT, preferred_element_type=F32)
    totals = [jnp.zeros((4, width), F32) for _ in range(out.shape[0])]
    for k in range(slots):
        channel = chan_of[k]
        beamed = sums[4 * k : 4 * k + 4] * (beam_s[pl.ds(channel, 1), :] * keep)
        for c in range(len(totals)):
            totals[c] = totals[c] + mixing[channel, c] * beamed
    for c in range(len(totals)):
        out[c, :, 0, :] = totals[c]


def body(
    comp_alms,
    legendre,
    inv_noise,
    beam_window,
    mixing,
    channel_of,
    m_orders,
    cycle_of,
    cycle_pixels,
    interpret=False,
    chan=lambda: lax.axis_index("chan"),
    blk=lambda: lax.axis_index("blk"),
    move=lambda x, axis: lax.all_to_all(x, axis, 0, 0, tiled=True),
):
    slots = channel_of.shape[0]
    orders = m_orders.shape[0]
    cycles = legendre.shape[3]
    width = comp_alms.shape[3]
    where = dict(chan=chan, blk=blk)
    partial = pl.pallas_call(
        functools.partial(forward_kernel, **where),
        out_shape=jax.ShapeDtypeStruct((slots, 4, cycles), F32),
        in_specs=[SMEM, SMEM, SMEM, VMEM, ANY, ANY],
        out_specs=VMEM,
        scratch_shapes=[
            pltpu.VMEM((beam_window.shape[0], width), F32),
            pltpu.VMEM((2 * width, cycles), BF16),
            pltpu.VMEM((slots * 4, 2 * width), F32),
            pltpu.SemaphoreType.DMA((3,)),
        ],
        interpret=interpret,
        name="forward",
    )(channel_of, mixing, m_orders, comp_alms, beam_window, legendre)
    pieces = move(partial, "chan")
    coeffs = jnp.sum(pieces, axis=0).astype(BF16)
    coeffs = move(jnp.broadcast_to(coeffs, (orders, 4, cycles)), "blk")
    held = inv_noise.shape[2]
    tall = inv_noise.shape[3] // LANES
    noise = inv_noise.reshape(2, held, tall, LANES).transpose(0, 2, 1, 3).reshape(2 * tall * held, LANES)
    grads = pl.pallas_call(
        functools.partial(cycle_kernel, blk=blk, slots=held),
        out_shape=jax.ShapeDtypeStruct((orders, 4, cycles), BF16),
        in_specs=[SMEM, SMEM, SMEM, VMEM, VMEM],
        out_specs=VMEM,
        interpret=interpret,
        name="cycles",
    )(cycle_of, cycle_pixels, m_orders, coeffs, noise)
    grads = jnp.sum(move(grads, "blk").astype(F32), axis=0).astype(BF16)
    grads = move(jnp.broadcast_to(grads, (slots, 4, cycles)), "chan")
    return pl.pallas_call(
        functools.partial(adjoint_kernel, **where),
        out_shape=jax.ShapeDtypeStruct(comp_alms.shape, F32),
        in_specs=[SMEM, SMEM, SMEM, VMEM, ANY, ANY],
        out_specs=VMEM,
        scratch_shapes=[
            pltpu.VMEM((beam_window.shape[0], width), F32),
            pltpu.VMEM((2, width, cycles), BF16),
            pltpu.SemaphoreType.DMA((3,)),
        ],
        interpret=interpret,
        name="adjoint",
    )(channel_of, mixing, m_orders, grads, beam_window, legendre)


def solution(mesh):
    placed = (
        P(None, None, "blk", "chan"),
        P(None, "blk", None, None),
        P("chan", None, "blk", None),
        P(),
        P(),
        P(),
        P(),
        P(),
        P(),
    )
    return jax.shard_map(
        body, mesh=mesh, in_specs=placed, out_specs=P(None, None, "blk", "chan"), check_vma=False
    )
```

time: 196 us -> 73.1 us (0.37)
  other arithmetic: 65.3 us -> 0.07 us
  blocking collectives: 17.6 us -> 63.4 us
  starting transfers between devices: 29.4 us -> 0 us
  matrix products: 27.7 us -> 0 us
  waiting for transfers between devices: 19.3 us -> 0 us
  local copies, waits for them, and re-layouts: 18.2 us -> 1.37 us
  loops' own time: 13.3 us -> 0 us
  Pallas kernels: 0 us -> 7.73 us
  between operations: 2.85 us -> 0.01 us
    another operation x10 -> x0, other arithmetic: 57.3 us -> none
    all_to_all x2 -> x4, blocking collectives: 17.6 us -> 63.4 us  [body(): lax.all_to_all(x, axis, 0, 0, tiled=True)]
    all_to_all x3 -> x0, starting transfers between devices: 29.4 us -> none  [the longest x1 15.4 us: body(): lax.all_to_all(slot_coeffs, 'blk', split_axis=3, concat_axis=2, tiled=True)]
    dot_general x29 -> x0, matrix products: 27.7 us -> none  [the longest x6 6.36 us: add_degrees(): lax.dot_general(twisted, tables[1, 0], (((1,), (1,)), ((), ())), preferre...]
    all_to_all x3 -> x0, waiting for transfers between devices: 19.3 us -> none  [the longest x1 8.61 us: body(): lax.all_to_all(slot_grads, 'blk', split_axis=2, concat_axis=3, tiled=True)]
    another operation x3 -> x0, loops' own time: 13.3 us -> none  [the longest x1 13.2 us: body(): lax.fori_loop(0, cycle_dev, per_cycle, jnp.zeros(by_cycle.shape, jnp.bflo...]
    dynamic_slice x14 -> x0, local copies, waits for them, and re-layouts: 10.2 us -> none  [the longest x8 4.89 us: per_cycle(): pix_count = cycle_pixels[cycle_of[first_slot + index]]]
    pallas_call x0 -> x3, Pallas kernels: none -> 7.73 us  [the longest x1 2.69 us: body(): pl.pallas_call(functools.partial(cycle_kernel, blk=blk, slots=held), out_...]
  transfers between devices with their start and end apart: 3 -> 0, of which waited for: 3 -> 0; matrix products, arithmetic and copies ran while one was open for 2% -> 0% of each run, Pallas kernels for 0% -> 0%
where the time goes in v1:
time: 73.1 us; the launch traced here: 72.6 us
  blocking collectives  63.4 us (87%)
  Pallas kernels  7.73 us (11%)
  local copies, waits for them, and re-layouts  1.37 us (2%)
    all_to_all x4, blocking collectives, body(): lax.all_to_all(x, axis, 0, 0, tiled=True)  63.4 us
    pallas_call x1, Pallas kernels, body(): pl.pallas_call(functools.partial(cycle_kernel, blk=blk, slots=held), out_...  2.69 us
    pallas_call x1, Pallas kernels, body(): pl.pallas_call(functools.partial(adjoint_kernel, **where), out_shape=jax....  2.55 us
    pallas_call x1, Pallas kernels, body(): pl.pallas_call(functools.partial(forward_kernel, **where), out_shape=jax....  2.49 us

profile of v1, /device:TPU:1, one launch (start us, length us, event | category | flops | bytes accessed | tf_op | source)
XLA Modules:
  0.0 72.6 jit_solution(1080949691879949874)
XLA Ops:
  0.0 1.3 %copy.12.mixing = f32[16,3]{1,0:T(8,128)} copy(f32[16,3]{0,1:T(4,128)} %param.13) | data formatting | bytes 384 | tf_op args[4]
  1.4 2.5 %forward.1 = f32[16,4,128]{2,1,0:T(4,128)} custom-call(s32[16]{0:T(128)} %chan_of.3, f32[16,3]{1,0:T(8,128)} %copy.12.mixing, s32[32]{0:T(128)} %orders.5, f32[3,4,1,256]{3,2,1,0:T(1,128)} %comp.1, f32[16,4096]{1,0:T(8,128)} %beam.3, bf16[2,1,4096,128]{3,2,1,0:T(8,128)(2,1)} %legendre.3), custom_call_target="tpu_custom_call" | custom-call | tf_op jit(solution)/shard_map/forward/pallas_call | solution.py:209
  3.8 17.6 %all_to_all.20 = f32[16,4,128]{2,1,0:T(4,128)S(1)} all-to-all(f32[16,4,128]{2,1,0:T(4,128)} %forward.1), channel_id=1, replica_groups=mesh['chan'=16,'blk'=32] {'chan'}, dimensions={0} | all-to-all | bytes 65536 | tf_op jit(solution)/shard_map/all_to_all | solution.py:202
  21.5 19.9 %all_to_all.21.coeffs = bf16[32,4,128]{2,1,0:T(4,128)(2,1)} all-to-all(bf16[32,4,128]{2,1,0:T(4,128)(2,1)S(1)} %broadcast_in_dim.6), channel_id=1, replica_groups=mesh['chan'=16,'blk'=32] {'blk'}, dimensions={0} | all-to-all | bytes 65536 | tf_op jit(solution)/shard_map/all_to_all | solution.py:202
  41.4 2.7 %cycles.1 = bf16[32,4,128]{2,1,0:T(4,128)(2,1)} custom-call(s32[128]{0:T(128)} %cycle_of.1, s32[128]{0:T(128)} %cycle_pixels.1, s32[32]{0:T(128)} %orders.5, bf16[32,4,128]{2,1,0:T(4,128)(2,1)} %all_to_all.21.coeffs, f32[512,128]{1,0:T(8,128)} %bitcast.5), custom_call_target="tpu_custom_call" | custom-call | tf_op jit(solution)/shard_map/cycles/pallas_call | solution.py:229
  44.1 12.4 %all_to_all.22 = bf16[32,4,128]{2,1,0:T(4,128)(2,1)S(1)} all-to-all(bf16[32,4,128]{2,1,0:T(4,128)(2,1)} %cycles.1), channel_id=1, replica_groups=mesh['chan'=16,'blk'=32] {'blk'}, dimensions={0} | all-to-all | bytes 65536 | tf_op jit(solution)/shard_map/all_to_all | solution.py:202
  56.6 13.4 %all_to_all.23.grads = bf16[16,4,128]{2,1,0:T(4,128)(2,1)} all-to-all(bf16[16,4,128]{2,1,0:T(4,128)(2,1)S(1)} %broadcast_in_dim.7), channel_id=1, replica_groups=mesh['chan'=16,'blk'=32] {'chan'}, dimensions={0} | all-to-all | bytes 32768 | tf_op jit(solution)/shard_map/all_to_all | solution.py:202
  70.0 2.5 %adjoint.1 = f32[3,4,1,256]{3,2,1,0:T(1,128)} custom-call(s32[16]{0:T(128)} %chan_of.3, f32[16,3]{1,0:T(8,128)} %copy.12.mixing, s32[32]{0:T(128)} %orders.5, bf16[16,4,128]{2,1,0:T(4,128)(2,1)} %all_to_all.23.grads, f32[16,4096]{1,0:T(8,128)} %beam.3, bf16[2,1,4096,128]{3,2,1,0:T(8,128)(2,1)} %legendre.3), custom_call_target="tpu_custom_call" | custom-call | tf_op jit(solution)/shard_map/adjoint/pallas_call | solution.py:239
  (4 shorter events, 0.1 us)

commit v2 on v1

v2 whole, which is shorter than its diff:
```python
import functools

import jax
import jax.numpy as jnp
from jax import lax
from jax.experimental import pallas as pl
from jax.experimental.pallas import tpu as pltpu
from jax.sharding import PartitionSpec as P

F32 = jnp.float32
BF16 = jnp.bfloat16
LANES = 128
NT = (((1,), (1,)), ((), ()))
TN = (((0,), (0,)), ((), ()))
NN = (((1,), (0,)), ((), ()))
COS = (0.9999999887921183, -19.739204415555925, 64.93911321613162, -85.45006149635309,
       60.16698573653733, -25.965151588112157, 6.525190124026944)
SIN = (6.28318530240345, -41.341700371179485, 81.60512965170976, -76.70298335354587,
       42.02566158843437, -14.898837201069828, 3.2367039052082127)

SMEM = pl.BlockSpec(memory_space=pltpu.SMEM)
VMEM = pl.BlockSpec(memory_space=pltpu.VMEM)
ANY = pl.BlockSpec(memory_space=pl.ANY)


def move(x, axis):
    return lax.all_to_all(x, axis, 0, 0, tiled=True)


def in_vmem(x):
    return pltpu.with_memory_space_constraint(x, pltpu.VMEM)


def nearest(x):
    return jnp.floor(x + 0.5)


def poly(z, terms):
    total = jnp.full_like(z, terms[-1])
    for term in terms[-2::-1]:
        total = total * z + term
    return total


def cos_turns(y):
    return poly(y * y, COS)


def sin_turns(y):
    return y * poly(y * y, SIN)


def turns_of(steps, period):
    inverse = 1.0 / period
    rest = steps - nearest(steps * inverse) * period
    return rest * inverse


def forward_kernel(
    chan_of, mixing, orders, comp, beam, legendre, out, comp_s, beam_s, leg_s, alm_s, sems, *, chan, blk
):
    width = comp.shape[3]
    first = chan() * width
    copies = [
        pltpu.make_async_copy(beam.at[:, pl.ds(first, width)], beam_s, sems.at[0]),
        pltpu.make_async_copy(legendre.at[0, 0, pl.ds(first, width), :], leg_s.at[pl.ds(0, width)], sems.at[1]),
        pltpu.make_async_copy(legendre.at[1, 0, pl.ds(first, width), :], leg_s.at[pl.ds(width, width)], sems.at[2]),
        pltpu.make_async_copy(comp, comp_s, sems.at[3]),
    ]
    for copy in copies:
        copy.start()
    order = orders[blk()]
    degrees = first + lax.broadcasted_iota(jnp.int32, (1, width), 1)
    keep = jnp.where(degrees >= order, 1.0, 0.0)
    copies[3].wait()
    parts = [comp_s[c, :, 0, :] * keep for c in range(comp.shape[0])]
    copies[0].wait()
    for k in range(out.shape[0]):
        channel = chan_of[k]
        mixed = mixing[0, channel] * parts[0]
        for c in range(1, len(parts)):
            mixed = mixed + mixing[c, channel] * parts[c]
        alm = mixed * beam_s[pl.ds(channel, 1), :]
        twisted = jnp.concatenate([-alm[3:4], alm[2:3], alm[1:2], -alm[0:1]], axis=0)
        alm_s[4 * k : 4 * k + 4, :width] = alm
        alm_s[4 * k : 4 * k + 4, width:] = twisted
    copies[1].wait()
    copies[2].wait()
    sums = lax.dot_general(alm_s[...].astype(BF16), leg_s[...], NN, preferred_element_type=F32)
    out[...] = sums.reshape(out.shape)


def lanes_of():
    lane = lax.broadcasted_iota(jnp.int32, (8, LANES), 1)
    return lane, lane % 2 == 1, lane % 4 < 2


def table_kernel(
    chan_of, mixing, orders, cycle_of, cycle_pixels, beam, legendre, noise,
    leg_out, mixed_out, pick_out, cos_out, sin_out, phase_out, weight_out,
    beam_s, noise_s, sems, *, chan, blk, slots
):
    width = leg_out.shape[1]
    first = chan() * width
    copies = [
        pltpu.make_async_copy(beam.at[:, pl.ds(first, width)], beam_s, sems.at[0]),
        pltpu.make_async_copy(noise, noise_s, sems.at[1]),
        pltpu.make_async_copy(legendre.at[0, 0, pl.ds(first, width), :], leg_out.at[0], sems.at[2]),
        pltpu.make_async_copy(legendre.at[1, 0, pl.ds(first, width), :], leg_out.at[1], sems.at[3]),
    ]
    for copy in copies:
        copy.start()
    count = orders.shape[0]
    lane, odd8, _ = lanes_of()
    order_row = jnp.zeros((8, LANES), F32)
    for i in range(count):
        order_row = jnp.where(lane // 4 == i, orders[i].astype(F32), order_row)
    m = order_row[:1]
    quarter = jnp.where(odd8[:1], 0.25, 0.0)
    start = blk() * slots
    cycles = [cycle_of[start + r] for r in range(slots)]
    row8 = lax.broadcasted_iota(jnp.int32, (8, LANES), 0)
    chosen8 = jnp.full((8, LANES), -1, jnp.int32)
    for r in range(slots):
        chosen8 = jnp.where(row8 == r, cycles[r], chosen8)
    pick_out[...] = jnp.where(lane == chosen8, 1.0, 0.0)
    half = noise.shape[0] // 2
    tall = half // slots
    steps_a = lax.broadcasted_iota(jnp.int32, (tall, LANES), 0).astype(F32) * m * 32.0
    steps_b = (2 * lax.broadcasted_iota(jnp.int32, (LANES, LANES), 0) + 1).astype(F32) * m
    pixel = (
        lax.broadcasted_iota(jnp.int32, (tall, LANES), 0) * LANES
        + lax.broadcasted_iota(jnp.int32, (tall, LANES), 1)
    )
    numbers = [cycle_pixels[cycles[r]] for r in range(slots)]
    for r in range(slots):
        number = jnp.full((1, LANES), numbers[r], jnp.int32).astype(F32)
        ya = turns_of(steps_a, number * 0.25)
        ya = ya - nearest(ya)
        cos_out[r] = cos_turns(ya)
        sin_out[r] = sin_turns(ya)
        yb = turns_of(steps_b, number * 2.0) - quarter
        yb = yb - nearest(yb)
        phase_out[r] = cos_turns(yb).astype(BF16)
    order = orders[blk()]
    degrees = first + lax.broadcasted_iota(jnp.int32, (1, width), 1)
    keep = jnp.where(degrees >= order, 1.0, 0.0)
    copies[0].wait()
    for k in range(chan_of.shape[0]):
        channel = chan_of[k]
        row = beam_s[pl.ds(channel, 1), :] * keep
        for c in range(mixed_out.shape[0]):
            mixed_out[c, 4 * k : 4 * k + 4, :] = jnp.broadcast_to(mixing[c, channel] * row, (4, width))
    copies[1].wait()
    for r in range(slots):
        inverse = 1.0 / jnp.full((1, LANES), numbers[r], jnp.int32).astype(F32)
        live = jnp.where(pixel < numbers[r], inverse, 0.0)
        weight_out[r, :tall] = noise_s[pl.ds(r, tall, stride=slots), :] * live
        weight_out[r, tall:] = noise_s[pl.ds(half + r, tall, stride=slots), :] * live
    copies[2].wait()
    copies[3].wait()


def cycle_kernel(coeffs, picked, cosines, sines, phases, weights, out):
    _, odd8, is_q8 = lanes_of()
    is_q = is_q8[:1]
    sign8 = jnp.where(odd8, -1.0, 1.0)
    row8 = lax.broadcasted_iota(jnp.int32, (8, LANES), 0)

    def swap(x):
        up = pltpu.roll(x, LANES - 1, 1)
        down = pltpu.roll(x, 1, 1)
        return jnp.where(odd8, down, up)

    slots, tall = cosines.shape[:2]
    pick = picked[...].astype(BF16)
    table = coeffs[...].reshape(LANES, LANES)
    x = lax.dot_general(pick, table, NT, preferred_element_type=F32)
    x_sign = x * sign8
    x_swap = swap(x)
    total_cos = jnp.zeros((8, LANES), F32)
    total_sin = jnp.zeros((8, LANES), F32)
    for r in range(slots):
        left = x_sign[r : r + 1] * cosines[r] - x_swap[r : r + 1] * sines[r]
        left = jnp.concatenate([jnp.where(is_q, left, 0.0), jnp.where(is_q, 0.0, left)], axis=0)
        maps = lax.dot_general(left.astype(BF16), phases[r], NT, preferred_element_type=F32)
        weighted = (weights[r] * maps).astype(BF16)
        back = lax.dot_general(weighted, phases[r], NN, preferred_element_type=F32)
        back = jnp.where(is_q, back[:tall], back[tall:])
        total_cos = jnp.where(row8 == r, jnp.sum(cosines[r] * back, axis=0, keepdims=True), total_cos)
        total_sin = jnp.where(row8 == r, jnp.sum(sines[r] * back, axis=0, keepdims=True), total_sin)
    grads = sign8 * total_cos - swap(total_sin)
    spread = lax.dot_general(grads.astype(BF16), pick, TN, preferred_element_type=F32)
    out[...] = spread.astype(BF16).reshape(out.shape)


def adjoint_kernel(grads, legendre, mixed, out):
    slots = grads.shape[0]
    straight = grads[...].astype(F32).reshape(slots * 4, LANES)
    row = lax.broadcasted_iota(jnp.int32, straight.shape, 0) % 4
    up = pltpu.roll(straight, straight.shape[0] - 1, 0)
    down = pltpu.roll(straight, 1, 0)
    up3 = pltpu.roll(straight, straight.shape[0] - 3, 0)
    down3 = pltpu.roll(straight, 3, 0)
    twisted = jnp.where(row == 0, -up3, jnp.where(row == 1, up, jnp.where(row == 2, down, -down3)))
    sums = lax.dot_general(straight.astype(BF16), legendre[0], NT, preferred_element_type=F32)
    sums = sums + lax.dot_general(twisted.astype(BF16), legendre[1], NT, preferred_element_type=F32)
    for c in range(out.shape[0]):
        pairs = jnp.sum((sums * mixed[c]).reshape(slots // 2, 8, sums.shape[1]), axis=0)
        out[c, :, 0, :] = pairs[:4] + pairs[4:]


def body(
    comp_alms,
    legendre,
    inv_noise,
    beam_window,
    mixing,
    channel_of,
    m_orders,
    cycle_of,
    cycle_pixels,
):
    slots = channel_of.shape[0]
    orders = m_orders.shape[0]
    cycles = legendre.shape[3]
    comps, _, _, width = comp_alms.shape
    where = dict(chan=lambda: lax.axis_index("chan"), blk=lambda: lax.axis_index("blk"))
    by_comp = mixing.T
    partial = pl.pallas_call(
        functools.partial(forward_kernel, **where),
        out_shape=pltpu.VMEM((slots, 4, cycles), F32),
        in_specs=[SMEM, SMEM, SMEM, ANY, ANY, ANY],
        out_specs=VMEM,
        scratch_shapes=[
            pltpu.VMEM(comp_alms.shape, F32),
            pltpu.VMEM((beam_window.shape[0], width), F32),
            pltpu.VMEM((2 * width, cycles), BF16),
            pltpu.VMEM((slots * 4, 2 * width), F32),
            pltpu.SemaphoreType.DMA((4,)),
        ],
        name="forward",
    )(channel_of, by_comp, m_orders, comp_alms, beam_window, legendre)
    pieces = move(partial, "chan")
    coeffs = jnp.sum(pieces, axis=0).astype(BF16)
    coeffs = move(jnp.broadcast_to(coeffs, (orders, 4, cycles)), "blk")
    held = inv_noise.shape[2]
    tall = inv_noise.shape[3] // LANES
    noise = inv_noise.reshape(2, held, tall, LANES).transpose(0, 2, 1, 3).reshape(2 * tall * held, LANES)
    legs, mixed, *tables = pl.pallas_call(
        functools.partial(table_kernel, slots=held, **where),
        out_shape=[
            pltpu.VMEM((2, width, cycles), BF16),
            pltpu.VMEM((comps, 4 * slots, width), F32),
            pltpu.VMEM((8, LANES), F32),
            pltpu.VMEM((held, tall, LANES), F32),
            pltpu.VMEM((held, tall, LANES), F32),
            pltpu.VMEM((held, LANES, LANES), BF16),
            pltpu.VMEM((held, 2 * tall, LANES), F32),
        ],
        in_specs=[SMEM, SMEM, SMEM, SMEM, SMEM, ANY, ANY, ANY],
        out_specs=[VMEM] * 7,
        scratch_shapes=[
            pltpu.VMEM((beam_window.shape[0], width), F32),
            pltpu.VMEM(noise.shape, F32),
            pltpu.SemaphoreType.DMA((4,)),
        ],
        name="tables",
    )(channel_of, by_comp, m_orders, cycle_of, cycle_pixels, beam_window, legendre, noise)
    grads = pl.pallas_call(
        cycle_kernel,
        out_shape=pltpu.VMEM((orders, 4, cycles), BF16),
        in_specs=[VMEM] * 6,
        out_specs=VMEM,
        name="cycles",
    )(in_vmem(coeffs), *map(in_vmem, tables))
    grads = jnp.sum(move(grads, "blk").astype(F32), axis=0).astype(BF16)
    grads = move(jnp.broadcast_to(grads, (slots, 4, cycles)), "chan")
    return pl.pallas_call(
        adjoint_kernel,
        out_shape=jax.ShapeDtypeStruct(comp_alms.shape, F32),
        in_specs=[VMEM] * 3,
        out_specs=VMEM,
        name="adjoint",
    )(in_vmem(grads), in_vmem(legs), in_vmem(mixed))


def solution(mesh):
    placed = (
        P(None, None, "blk", "chan"),
        P(None, "blk", None, None),
        P("chan", None, "blk", None),
        P(),
        P(),
        P(),
        P(),
        P(),
        P(),
    )
    return jax.shard_map(
        body, mesh=mesh, in_specs=placed, out_specs=P(None, None, "blk", "chan"), check_vma=False
    )
```

time: 73.1 us -> 66.5 us (0.910)
  blocking collectives: 63.4 us -> 41.1 us
  starting transfers between devices: 0 us -> 11.9 us
  waiting for transfers between devices: 0 us -> 6.92 us
  Pallas kernels: 7.73 us -> 5.43 us
  local copies, waits for them, and re-layouts: 1.37 us -> 0.62 us
    all_to_all x4 -> x3, blocking collectives: 63.4 us -> 41.1 us  [move(): return lax.all_to_all(x, axis, 0, 0, tiled=True)]
    all_to_all x0 -> x1, starting transfers between devices: none -> 11.9 us  [move(): return lax.all_to_all(x, axis, 0, 0, tiled=True)]
    all_to_all x0 -> x1, waiting for transfers between devices: none -> 6.92 us  [move(): return lax.all_to_all(x, axis, 0, 0, tiled=True)]
    pallas_call x3 -> x4, Pallas kernels: 7.73 us -> 5.43 us  [the longest x1 1.79 us: body(): pl.pallas_call(functools.partial(forward_kernel, **where), out_shape=pltp...]
    unnamed x1 -> x0, local copies, waits for them, and re-layouts: 1.35 us -> none
  transfers between devices with their start and end apart: 0 -> 1, of which waited for: 0 -> 1; matrix products, arithmetic and copies ran while one was open for 0% -> 0% of each run, Pallas kernels for 0% -> 3%
where the time goes in v2:
time: 66.5 us; the launch traced here: 66.1 us
  blocking collectives  41.1 us (62%)
  starting transfers between devices  11.9 us (18%)
  waiting for transfers between devices  6.92 us (10%)
  Pallas kernels  5.43 us (8%)
    all_to_all x3, blocking collectives, move(): return lax.all_to_all(x, axis, 0, 0, tiled=True)  41.1 us
    all_to_all x1, starting transfers between devices, move(): return lax.all_to_all(x, axis, 0, 0, tiled=True)  11.9 us
    all_to_all x1, waiting for transfers between devices, move(): return lax.all_to_all(x, axis, 0, 0, tiled=True)  6.92 us
    pallas_call x1, Pallas kernels, body(): pl.pallas_call(functools.partial(forward_kernel, **where), out_shape=pltp...  1.79 us
    pallas_call x1, Pallas kernels, body(): pl.pallas_call(functools.partial(table_kernel, slots=held, **where), out_...  1.77 us
  transfers between devices with their start and end apart: 1, of which 1 were waited for; matrix products, arithmetic and copies ran while one was open for 0% of the time, Pallas kernels for 3%

profile of v2, /device:TPU:1, one launch (start us, length us, event | category | flops | bytes accessed | tf_op | source)
XLA Modules:
  0.0 66.1 jit_solution(699461598271916525)
XLA Ops:
  0.0 1.8 %forward.1 = f32[16,4,128]{2,1,0:T(4,128)S(1)} custom-call(s32[16]{0:T(128)} %chan_of.3, f32[3,16]{1,0:T(4,128)} %bitcast.7, s32[32]{0:T(128)} %orders.3, f32[3,4,1,256]{3,2,1,0:T(1,128)} %comp.1, f32[16,4096]{1,0:T(8,128)} %beam.3, bf16[2,1,4096,128]{3,2,1,0:T(8,128)(2,1)} %legendre.3), custom_call_target="tpu_custom_call" | custom-call | tf_op jit(solution)/shard_map/forward/pallas_call | solution.py:230
  1.8 16.7 %all_to_all.20 = f32[16,4,128]{2,1,0:T(4,128)S(1)} all-to-all(f32[16,4,128]{2,1,0:T(4,128)S(1)} %forward.1), channel_id=1, replica_groups=mesh['chan'=16,'blk'=32] {'chan'}, dimensions={0} | all-to-all | bytes 65536 | tf_op jit(solution)/shard_map/all_to_all | solution.py:27
  18.6 0.6 broadcast_in_dim.6
  19.2 11.9 %all-to-all-start.1 = ((bf16[32,4,128]{2,1,0:T(4,128)(2,1)}), bf16[32,4,128]{2,1,0:T(4,128)(2,1)S(1)}, u32[]{:S(2)}, u32[]{:S(2)}) async-start(bf16[32,4,128]{2,1,0:T(4,128)(2,1)} %broadcast_in_dim.6), calls=%async_computation.1 | async-start | bytes 65536 | tf_op jit(solution)/shard_map/all_to_all | solution.py:27
  31.1 1.8 %tables.1 = (bf16[2,256,128]{2,1,0:T(8,128)(2,1)S(1)}, f32[3,64,256]{2,1,0:T(8,128)S(1)}, f32[8,128]{1,0:T(8,128)S(1)}, f32[4,64,128]{2,1,0:T(8,128)S(1)}, f32[4...) custom-call(s32[16]{0:T(128)} %chan_of.3, f32[3,16]{1,0:T(4,128)} %bitcast.8, ...), custom_call_target="tpu_custom_call" | custom-call | tf_op jit(solution)/shard_map/tables/pallas_call | solution.py:250
  32.9 6.9 %all-to-all-done.1.coeffs = bf16[32,4,128]{2,1,0:T(4,128)(2,1)S(1)} async-done(((bf16[32,4,128]{2,1,0:T(4,128)(2,1)}), bf16[32,4,128]{2,1,0:T(4,128)(2,1)S(1)}, u32[]{:S(2)}, u32[]{:S(2)}) %all-to-all-start.1) | async-done | bytes 32800 | tf_op jit(solution)/shard_map/all_to_all | solution.py:27
  39.8 1.1 %cycles.1 = bf16[32,4,128]{2,1,0:T(4,128)(2,1)S(1)} custom-call(bf16[32,4,128]{2,1,0:T(4,128)(2,1)S(1)} %all-to-all-done.1.coeffs, f32[8,128]{1,0:T(8,128)S(1)} %get-tuple-element.12.picked, f32[4,64,128]{2,1,0:T(8,128)S(1)} %get-tuple-element.13.cosines, f32[4,64,128]{2,1,0:T(8,128)S(1)} %get-tuple-element.14.sines, ...), custom_call_target="tpu_custom_call" | custom-call | tf_op jit(solution)/shard_map/cycles/pallas_call | solution.py:270
  40.9 11.6 %all_to_all.21 = bf16[32,4,128]{2,1,0:T(4,128)(2,1)S(1)} all-to-all(bf16[32,4,128]{2,1,0:T(4,128)(2,1)S(1)} %cycles.1), channel_id=1, replica_groups=mesh['chan'=16,'blk'=32] {'blk'}, dimensions={0} | all-to-all | bytes 65536 | tf_op jit(solution)/shard_map/all_to_all | solution.py:27
  52.6 12.8 %all_to_all.22.grads = bf16[16,4,128]{2,1,0:T(4,128)(2,1)S(1)} all-to-all(bf16[16,4,128]{2,1,0:T(4,128)(2,1)S(1)} %broadcast_in_dim.7), channel_id=1, replica_groups=mesh['chan'=16,'blk'=32] {'chan'}, dimensions={0} | all-to-all | bytes 32768 | tf_op jit(solution)/shard_map/all_to_all | solution.py:27
  65.3 0.8 %adjoint.1 = f32[3,4,1,256]{3,2,1,0:T(1,128)} custom-call(bf16[16,4,128]{2,1,0:T(4,128)(2,1)S(1)} %all_to_all.22.grads, bf16[2,256,128]{2,1,0:T(8,128)(2,1)S(1)} %get-tuple-element.17.legendre, f32[3,64,256]{2,1,0:T(8,128)S(1)} %get-tuple-element.18.mixed), custom_call_target="tpu_custom_call" | custom-call | tf_op jit(solution)/shard_map/adjoint/pallas_call | solution.py:279
  (3 shorter events, 0.1 us)
Async XLA Ops:
  19.2 20.6 %all-to-all-start.1 = ((bf16[32,4,128]{2,1,0:T(4,128)(2,1)}), bf16[32,4,128]{2,1,0:T(4,128)(2,1)S(1)}, u32[]{:S(2)}, u32[]{:S(2)}) async-start(bf16[32,4,128]{2,1,0:T(4,128)(2,1)} %broadcast_in_dim.6), calls=%async_computation.1 | async-start | bytes 65536 | tf_op jit(solution)/shard_map/all_to_all | solution.py:27

commit v3 on v2

v3 whole, which is shorter than its diff:
```python
import functools

import jax
import jax.numpy as jnp
from jax import lax
from jax.experimental import pallas as pl
from jax.experimental.pallas import tpu as pltpu
from jax.sharding import PartitionSpec as P

F32 = jnp.float32
BF16 = jnp.bfloat16
LANES = 128
NT = (((1,), (1,)), ((), ()))
NN = (((1,), (0,)), ((), ()))
COS = (0.9999999887921183, -19.739204415555925, 64.93911321613162, -85.45006149635309,
       60.16698573653733, -25.965151588112157, 6.525190124026944)
SIN = (6.28318530240345, -41.341700371179485, 81.60512965170976, -76.70298335354587,
       42.02566158843437, -14.898837201069828, 3.2367039052082127)

SMEM = pl.BlockSpec(memory_space=pltpu.SMEM)
VMEM = pl.BlockSpec(memory_space=pltpu.VMEM)
ANY = pl.BlockSpec(memory_space=pl.ANY)


def move(x, axis):
    return lax.all_to_all(x, axis, 0, 0, tiled=True)


def in_vmem(x):
    return pltpu.with_memory_space_constraint(x, pltpu.VMEM)


def nearest(x):
    return jnp.floor(x + 0.5)


def poly(z, terms):
    total = jnp.full_like(z, terms[-1])
    for term in terms[-2::-1]:
        total = total * z + term
    return total


def cos_turns(y):
    return poly(y * y, COS)


def sin_turns(y):
    return y * poly(y * y, SIN)


def turns_of(steps, period):
    inverse = 1.0 / period
    rest = steps - nearest(steps * inverse) * period
    return rest * inverse


def forward_kernel(
    chan_of, mixing, orders, comp, beam, legendre, out, leg, mixed_out, comp_s, beam_s, alm_s, sems, *, chan, blk
):
    width = comp.shape[3]
    first = chan() * width
    copies = [
        pltpu.make_async_copy(beam.at[:, pl.ds(first, width)], beam_s, sems.at[0]),
        pltpu.make_async_copy(legendre.at[0, 0, pl.ds(first, width), :], leg.at[pl.ds(0, width)], sems.at[1]),
        pltpu.make_async_copy(legendre.at[1, 0, pl.ds(first, width), :], leg.at[pl.ds(width, width)], sems.at[2]),
        pltpu.make_async_copy(comp, comp_s, sems.at[3]),
    ]
    for copy in copies:
        copy.start()
    order = orders[blk()]
    degrees = first + lax.broadcasted_iota(jnp.int32, (1, width), 1)
    keep = jnp.where(degrees >= order, 1.0, 0.0)
    copies[3].wait()
    parts = [comp_s[c, :, 0, :] for c in range(comp.shape[0])]
    copies[0].wait()
    for k in range(out.shape[0]):
        channel = chan_of[k]
        row = beam_s[pl.ds(channel, 1), :] * keep
        mixed = mixing[0, channel] * parts[0]
        for c in range(1, len(parts)):
            mixed = mixed + mixing[c, channel] * parts[c]
        alm = mixed * row
        twisted = jnp.concatenate([-alm[3:4], alm[2:3], alm[1:2], -alm[0:1]], axis=0)
        alm_s[4 * k : 4 * k + 4, :width] = alm
        alm_s[4 * k : 4 * k + 4, width:] = twisted
        for c in range(len(parts)):
            mixed_out[c, 4 * k : 4 * k + 4, :] = jnp.broadcast_to(mixing[c, channel] * row, (4, width))
    copies[1].wait()
    copies[2].wait()
    sums = lax.dot_general(alm_s[...].astype(BF16), leg[...], NN, preferred_element_type=F32)
    out[...] = sums.reshape(out.shape)


def cycle_matrix_kernel(
    orders, cycle_of, cycle_pixels, cycle_row, noise, out, pick_out, noise_s, weight_s, order_s, sems, *, blk, slots
):
    copy = pltpu.make_async_copy(noise, noise_s, sems.at[0])
    copy.start()
    count = orders.shape[0]
    start = blk() * slots
    numbers = [cycle_pixels[cycle_of[start + r]] for r in range(slots)]
    for i in range(count):
        order_s[i : i + 1, :] = jnp.full((1, LANES), orders[i], jnp.int32).astype(F32)
    m = order_s[...]
    square = (LANES, LANES)
    slot_of = lax.broadcasted_iota(jnp.int32, (2 * LANES, LANES), 0)
    slot_of = 4 * (slot_of // 8) + slot_of % 4
    expand = jnp.where(slot_of == lax.broadcasted_iota(jnp.int32, slot_of.shape, 1), 1.0, 0.0).astype(BF16)
    at_cycle = jnp.where(lax.broadcasted_iota(jnp.int32, square, 0) == cycle_row[...], 1.0, 0.0).astype(BF16)
    pick_out[...] = lax.dot_general(expand, at_cycle, NT, preferred_element_type=F32).astype(BF16)

    half = noise.shape[0] // 2
    tall = half // slots
    pixel = (
        lax.broadcasted_iota(jnp.int32, (tall, LANES), 0) * LANES
        + lax.broadcasted_iota(jnp.int32, (tall, LANES), 1)
    )
    copy.wait()
    for r in range(slots):
        inverse = 1.0 / jnp.full((1, LANES), numbers[r], jnp.int32).astype(F32)
        live = jnp.where(pixel < numbers[r], inverse, 0.0)
        weight_s[r, 0] = noise_s[pl.ds(r, tall, stride=slots), :] * live
        weight_s[r, 1] = noise_s[pl.ds(half + r, tall, stride=slots), :] * live

    source = lax.broadcasted_iota(jnp.int32, (2 * LANES, 1), 0)
    x, t, xx, ii = source // 128, source // 64 % 2, source // 32 % 2, source % 32
    target = (ii // 16) * 128 + (ii % 16) * 8 + x * 4 + t * 2 + xx
    value = jnp.where(x == xx, 1.0, -1.0)
    order_lanes = jnp.where(
        lax.broadcasted_iota(jnp.int32, (2 * LANES, 2 * LANES), 1) == target, value, 0.0
    ).astype(BF16)

    odd_steps = (2 * lax.broadcasted_iota(jnp.int32, (count, LANES), 1) + 1).astype(F32) * m
    unroll = 8
    for r in range(slots):
        number = jnp.full((1, LANES), numbers[r], jnp.int32).astype(F32)
        turn = turns_of(m * 32.0, number * 0.25)
        turn = turn - nearest(turn)
        turn_cos, turn_sin = cos_turns(turn), sin_turns(turn)
        base = turns_of(odd_steps, number * 2.0)
        base = base - nearest(base)

        def add_pixels(chunk, state, r=r, turn_cos=turn_cos, turn_sin=turn_sin):
            total, c, s = state
            first = pl.multiple_of(chunk * unroll, unroll)
            rows_q = weight_s[r, 0, pl.ds(first, unroll), :]
            rows_u = weight_s[r, 1, pl.ds(first, unroll), :]
            for pair in range(unroll // 2):
                phases, weighted = [], []
                for step in (2 * pair, 2 * pair + 1):
                    q, u = rows_q[step : step + 1], rows_u[step : step + 1]
                    phases.append(jnp.concatenate([c, s], axis=0).astype(BF16))
                    weighted.append(jnp.concatenate([q * c, q * s, u * c, u * s], axis=0).astype(BF16))
                    c, s = c * turn_cos - s * turn_sin, s * turn_cos + c * turn_sin
                total = total + lax.dot_general(
                    jnp.concatenate(phases, axis=1),
                    jnp.concatenate(weighted, axis=1),
                    NT,
                    preferred_element_type=F32,
                )
            return total, c, s

        total, _, _ = lax.fori_loop(
            0,
            tall // unroll,
            add_pixels,
            (jnp.zeros((2 * count, LANES), F32), cos_turns(base), sin_turns(base)),
        )
        pair = jnp.concatenate([total[:count], total[count:]], axis=1).astype(BF16)
        placed = lax.dot_general(pair, order_lanes, NN, preferred_element_type=F32)
        out[:, r, :] = placed[:, :LANES]
        out[:, slots + r, :] = placed[:, LANES:]


def join_kernel(pieces, matrix, out):
    coeffs = jnp.sum(pieces[...], axis=0)
    twice = jnp.concatenate([coeffs, coeffs], axis=0)
    for i in range(out.shape[0]):
        out[i] = jnp.concatenate([matrix[i], twice], axis=0).astype(BF16)


def cycle_kernel(received, pick, out):
    values = received[...].astype(F32)
    matrix = values[:, :8, :].reshape(2 * LANES, LANES)
    coeffs = values[:, 8:, :].reshape(2 * LANES, LANES).astype(BF16)
    picks = pick[...]
    low = lax.dot_general(picks, coeffs[:LANES], NT, preferred_element_type=F32)
    high = lax.dot_general(picks, coeffs[LANES:], NT, preferred_element_type=F32)
    upper = lax.broadcasted_iota(jnp.int32, low.shape, 0) % 8 >= 4
    product = matrix * jnp.where(upper, high, low)
    lane = lax.broadcasted_iota(jnp.int32, (8, LANES), 1)
    part = lane // 2 % 2 * 2 + lane // 4 % 2
    gather = jnp.where(part == lax.broadcasted_iota(jnp.int32, part.shape, 0), 1.0, 0.0).astype(BF16)

    def exact(dot, x):
        head = x.astype(BF16)
        return dot(head) + dot((x - head.astype(F32)).astype(BF16))

    by_slot = exact(lambda y: lax.dot_general(gather, y, NT, preferred_element_type=F32), product)
    grads = exact(lambda y: lax.dot_general(y, picks, NN, preferred_element_type=F32), by_slot)
    out[...] = jnp.broadcast_to(grads[:4].astype(BF16)[None], out.shape)


def adjoint_kernel(grads, legendre, mixed, out):
    slots = grads.shape[0]
    width = out.shape[3]
    straight = grads[...].astype(F32).reshape(slots * 4, LANES)
    row = lax.broadcasted_iota(jnp.int32, straight.shape, 0) % 4
    up = pltpu.roll(straight, straight.shape[0] - 1, 0)
    down = pltpu.roll(straight, 1, 0)
    up3 = pltpu.roll(straight, straight.shape[0] - 3, 0)
    down3 = pltpu.roll(straight, 3, 0)
    twisted = jnp.where(row == 0, -up3, jnp.where(row == 1, up, jnp.where(row == 2, down, -down3)))
    sums = lax.dot_general(straight.astype(BF16), legendre[:width], NT, preferred_element_type=F32)
    sums = sums + lax.dot_general(twisted.astype(BF16), legendre[width:], NT, preferred_element_type=F32)
    for c in range(out.shape[0]):
        pairs = jnp.sum((sums * mixed[c]).reshape(slots // 2, 8, sums.shape[1]), axis=0)
        out[c, :, 0, :] = pairs[:4] + pairs[4:]


def body(
    comp_alms,
    legendre,
    inv_noise,
    beam_window,
    mixing,
    channel_of,
    m_orders,
    cycle_of,
    cycle_pixels,
):
    slots = channel_of.shape[0]
    orders = m_orders.shape[0]
    cycles = legendre.shape[3]
    comps, _, _, width = comp_alms.shape
    chan = functools.partial(lax.axis_index, "chan")
    blk = functools.partial(lax.axis_index, "blk")
    partial, legs, mixed = pl.pallas_call(
        functools.partial(forward_kernel, chan=chan, blk=blk),
        out_shape=[
            jax.ShapeDtypeStruct((slots, 4, cycles), F32),
            pltpu.VMEM((2 * width, cycles), BF16),
            pltpu.VMEM((comps, 4 * slots, width), F32),
        ],
        in_specs=[SMEM, SMEM, SMEM, ANY, ANY, ANY],
        out_specs=[VMEM] * 3,
        scratch_shapes=[
            pltpu.VMEM(comp_alms.shape, F32),
            pltpu.VMEM((beam_window.shape[0], width), F32),
            pltpu.VMEM((slots * 4, 2 * width), F32),
            pltpu.SemaphoreType.DMA((4,)),
        ],
        name="forward",
    )(channel_of, mixing.T, m_orders, comp_alms, beam_window, legendre)
    pieces = move(partial, "chan")
    held = inv_noise.shape[2]
    tall = inv_noise.shape[3] // LANES
    noise = inv_noise.reshape(2, held, tall, LANES).transpose(0, 2, 1, 3).reshape(2 * tall * held, LANES)
    matrix, pick = pl.pallas_call(
        functools.partial(cycle_matrix_kernel, blk=blk, slots=held),
        out_shape=[pltpu.VMEM((orders, 2 * held, LANES), F32), pltpu.VMEM((2 * LANES, LANES), BF16)],
        in_specs=[SMEM, SMEM, SMEM, VMEM, ANY],
        out_specs=[VMEM] * 2,
        scratch_shapes=[
            pltpu.VMEM(noise.shape, F32),
            pltpu.VMEM((held, 2, tall, LANES), F32),
            pltpu.VMEM((orders, LANES), F32),
            pltpu.SemaphoreType.DMA((1,)),
        ],
        name="matrices",
    )(m_orders, cycle_of, cycle_pixels, cycle_of.reshape(1, -1), noise)
    message = pl.pallas_call(
        join_kernel,
        out_shape=pltpu.VMEM((orders, 16, LANES), BF16),
        in_specs=[VMEM] * 2,
        out_specs=VMEM,
        name="join",
    )(in_vmem(pieces), in_vmem(matrix))
    grads = pl.pallas_call(
        cycle_kernel,
        out_shape=pltpu.VMEM((slots, 4, cycles), BF16),
        in_specs=[VMEM] * 2,
        out_specs=VMEM,
        name="cycles",
    )(in_vmem(move(message, "blk")), in_vmem(pick))
    return pl.pallas_call(
        adjoint_kernel,
        out_shape=jax.ShapeDtypeStruct(comp_alms.shape, F32),
        in_specs=[VMEM] * 3,
        out_specs=VMEM,
        name="adjoint",
    )(in_vmem(move(grads, "chan")), in_vmem(legs), in_vmem(mixed))


def solution(mesh):
    placed = (
        P(None, None, "blk", "chan"),
        P(None, "blk", None, None),
        P("chan", None, "blk", None),
        P(),
        P(),
        P(),
        P(),
        P(),
        P(),
    )
    return jax.shard_map(
        body, mesh=mesh, in_specs=placed, out_specs=P(None, None, "blk", "chan"), check_vma=False
    )
```

time: 66.5 us -> 60.7 us (0.913)
  Pallas kernels: 5.43 us -> 13.6 us
  waiting for transfers between devices: 6.92 us -> 0.01 us
  blocking collectives: 41.1 us -> 36.6 us
  starting transfers between devices: 11.9 us -> 10.1 us
    pallas_call x3 -> x4, Pallas kernels: 4.64 us -> 12.8 us  [the longest x1 9.79 us: body(): pl.pallas_call(functools.partial(cycle_matrix_kernel, blk=blk, slots=held...]
    all_to_all x1, waiting for transfers between devices: 6.92 us -> 0.01 us  [move(): return lax.all_to_all(x, axis, 0, 0, tiled=True)]
    all_to_all x3 -> x2, blocking collectives: 41.1 us -> 36.6 us  [move(): return lax.all_to_all(x, axis, 0, 0, tiled=True)]
    all_to_all x1, starting transfers between devices: 11.9 us -> 10.1 us  [move(): return lax.all_to_all(x, axis, 0, 0, tiled=True)]
  transfers between devices with their start and end apart: 1 -> 1, of which waited for: 1 -> 0; matrix products, arithmetic and copies ran while one was open for 0% -> 0% of each run, Pallas kernels for 3% -> 16%
where the time goes in v3:
time: 60.7 us; the launch traced here: 60.3 us
  blocking collectives  36.6 us (60%)
  Pallas kernels  13.6 us (22%)
  starting transfers between devices  10.1 us (17%)
    all_to_all x2, blocking collectives, move(): return lax.all_to_all(x, axis, 0, 0, tiled=True)  36.6 us
    all_to_all x1, starting transfers between devices, move(): return lax.all_to_all(x, axis, 0, 0, tiled=True)  10.1 us
    pallas_call x1, Pallas kernels, body(): pl.pallas_call(functools.partial(cycle_matrix_kernel, blk=blk, slots=held...  9.79 us
    pallas_call x1, Pallas kernels, body(): pl.pallas_call(functools.partial(forward_kernel, chan=chan, blk=blk), out...  2.45 us
  transfers between devices with their start and end apart: 1, of which 0 were waited for; matrix products, arithmetic and copies ran while one was open for 0% of the time, Pallas kernels for 16%

profile of v3, /device:TPU:1, one launch (start us, length us, event | category | flops | bytes accessed | tf_op | source)
XLA Modules:
  0.0 60.3 jit_solution(3821921128444059335)
XLA Ops:
  0.0 2.5 %forward.1 = (f32[16,4,128]{2,1,0:T(4,128)}, bf16[512,128]{1,0:T(8,128)(2,1)S(1)}, f32[3,64,256]{2,1,0:T(8,128)S(1)}) custom-call(s32[16]{0:T(128)} %chan_of.1, f32[3,16]{1,0:T(4,128)} %bitcast.8, s32[32]{0:T(128)} %orders.3, f32[3,4,1,256]{3,2,1,0:T(1,128)} %comp.1, f32[16,4096]{1,0:T(8,128)} %beam.1, bf16[2,1,4096,128]{3,2,1,0:T(8,128)(2,1)} %legendre.1), custom_call_target="tpu_custom_call" | custom-call | tf_op jit(solution)/shard_map/forward/pallas_call | solution.py:239
  2.5 10.1 %all-to-all-start = ((f32[16,4,128]{2,1,0:T(4,128)}), f32[16,4,128]{2,1,0:T(4,128)S(1)}, u32[]{:S(2)}, u32[]{:S(2)}) async-start(f32[16,4,128]{2,1,0:T(4,128)} %get-tuple-element.10), calls=%async_computation | async-start | bytes 65536 | tf_op jit(solution)/shard_map/all_to_all | solution.py:26
  12.6 9.8 %matrices.1 = (f32[32,8,128]{2,1,0:T(8,128)S(1)}, bf16[256,128]{1,0:T(8,128)(2,1)S(1)}) custom-call(s32[32]{0:T(128)} %orders.3, s32[128]{0:T(128)} %cycle_of.1, s32[128]{0:T(128)} %cycle_pixels.1, s32[1,128]{1,0:T(1,128)} %bitcast.9, f32[512,128]{1,0:T(8,128)} %bitcast.7), custom_call_target="tpu_custom_call" | custom-call | tf_op jit(solution)/shard_map/matrices/pallas_call | solution.py:260
  22.4 0.0 all-to-all-done.pieces
  22.5 21.1 %all_to_all.15.received = bf16[32,16,128]{2,1,0:T(8,128)(2,1)S(1)} all-to-all(bf16[32,16,128]{2,1,0:T(8,128)(2,1)S(1)} %join.1), channel_id=1, replica_groups=mesh['chan'=16,'blk'=32] {'blk'}, dimensions={0} | all-to-all | bytes 262144 | tf_op jit(solution)/shard_map/all_to_all | solution.py:26
  43.5 0.5 cycles.1
  44.0 15.5 %all_to_all.16.grads = bf16[16,4,128]{2,1,0:T(4,128)(2,1)S(1)} all-to-all(bf16[16,4,128]{2,1,0:T(4,128)(2,1)S(1)} %cycles.1), channel_id=1, replica_groups=mesh['chan'=16,'blk'=32] {'chan'}, dimensions={0} | all-to-all | bytes 32768 | tf_op jit(solution)/shard_map/all_to_all | solution.py:26
  59.5 0.8 %adjoint.1 = f32[3,4,1,256]{3,2,1,0:T(1,128)} custom-call(bf16[16,4,128]{2,1,0:T(4,128)(2,1)S(1)} %all_to_all.16.grads, bf16[512,128]{1,0:T(8,128)(2,1)S(1)} %get-tuple-element.13.legendre, f32[3,64,256]{2,1,0:T(8,128)S(1)} %get-tuple-element.14.mixed), custom_call_target="tpu_custom_call" | custom-call | tf_op jit(solution)/shard_map/adjoint/pallas_call | solution.py:287
  (1 shorter events, 0.0 us)
Async XLA Ops:
  2.5 20.0 %all-to-all-start = ((f32[16,4,128]{2,1,0:T(4,128)}), f32[16,4,128]{2,1,0:T(4,128)S(1)}, u32[]{:S(2)}, u32[]{:S(2)}) async-start(f32[16,4,128]{2,1,0:T(4,128)} %get-tuple-element.10), calls=%async_computation | async-start | bytes 65536 | tf_op jit(solution)/shard_map/all_to_all | solution.py:26

commit v4 on v3

--- a/solution.py
+++ b/solution.py
@@ -17,7 +17,6 @@
 SIN = (6.28318530240345, -41.341700371179485, 81.60512965170976, -76.70298335354587,
        42.02566158843437, -14.898837201069828, 3.2367039052082127)
 
-SMEM = pl.BlockSpec(memory_space=pltpu.SMEM)
 VMEM = pl.BlockSpec(memory_space=pltpu.VMEM)
 ANY = pl.BlockSpec(memory_space=pl.ANY)
 
@@ -56,7 +55,8 @@
 
 
 def forward_kernel(
-    chan_of, mixing, orders, comp, beam, legendre, out, leg, mixed_out, comp_s, beam_s, alm_s, sems, *, chan, blk
+    chan_of_hbm, mixing_hbm, orders_hbm, comp, beam, legendre, out, leg, mixed_out,
+    chan_of, mixing, orders, comp_s, beam_s, alm_s, sems, *, chan, blk
 ):
     width = comp.shape[3]
     first = chan() * width
@@ -65,15 +65,18 @@
         pltpu.make_async_copy(legendre.at[0, 0, pl.ds(first, width), :], leg.at[pl.ds(0, width)], sems.at[1]),
         pltpu.make_async_copy(legendre.at[1, 0, pl.ds(first, width), :], leg.at[pl.ds(width, width)], sems.at[2]),
         pltpu.make_async_copy(comp, comp_s, sems.at[3]),
+        pltpu.make_async_copy(chan_of_hbm, chan_of, sems.at[4]),
+        pltpu.make_async_copy(mixing_hbm, mixing, sems.at[5]),
+        pltpu.make_async_copy(orders_hbm, orders, sems.at[6]),
     ]
-    for copy in copies:
+    for copy in copies[::-1]:
         copy.start()
+    degrees = first + lax.broadcasted_iota(jnp.int32, (1, width), 1)
+    for copy in (copies[0], *copies[3:]):
+        copy.wait()
     order = orders[blk()]
-    degrees = first + lax.broadcasted_iota(jnp.int32, (1, width), 1)
     keep = jnp.where(degrees >= order, 1.0, 0.0)
-    copies[3].wait()
     parts = [comp_s[c, :, 0, :] for c in range(comp.shape[0])]
-    copies[0].wait()
     for k in range(out.shape[0]):
         channel = chan_of[k]
         row = beam_s[pl.ds(channel, 1), :] * keep
@@ -93,36 +96,24 @@
 
 
 def cycle_matrix_kernel(
-    orders, cycle_of, cycle_pixels, cycle_row, noise, out, pick_out, noise_s, weight_s, order_s, sems, *, blk, slots
+    orders_hbm, cycle_of_hbm, cycle_pixels_hbm, cycle_row_hbm, noise, out, pick_out,
+    orders, cycle_of, cycle_pixels, cycle_row, noise_s, weight_s, order_s, sems, *, blk, slots
 ):
-    copy = pltpu.make_async_copy(noise, noise_s, sems.at[0])
-    copy.start()
+    pairs = (
+        (orders_hbm, orders),
+        (cycle_of_hbm, cycle_of),
+        (cycle_pixels_hbm, cycle_pixels),
+        (cycle_row_hbm, cycle_row),
+        (noise, noise_s),
+    )
+    copies = [pltpu.make_async_copy(src, dst, sems.at[n]) for n, (src, dst) in enumerate(pairs)]
+    for copy in copies:
+        copy.start()
     count = orders.shape[0]
     start = blk() * slots
-    numbers = [cycle_pixels[cycle_of[start + r]] for r in range(slots)]
-    for i in range(count):
-        order_s[i : i + 1, :] = jnp.full((1, LANES), orders[i], jnp.int32).astype(F32)
-    m = order_s[...]
-    square = (LANES, LANES)
     slot_of = lax.broadcasted_iota(jnp.int32, (2 * LANES, LANES), 0)
     slot_of = 4 * (slot_of // 8) + slot_of % 4
     expand = jnp.where(slot_of == lax.broadcasted_iota(jnp.int32, slot_of.shape, 1), 1.0, 0.0).astype(BF16)
-    at_cycle = jnp.where(lax.broadcasted_iota(jnp.int32, square, 0) == cycle_row[...], 1.0, 0.0).astype(BF16)
-    pick_out[...] = lax.dot_general(expand, at_cycle, NT, preferred_element_type=F32).astype(BF16)
-
-    half = noise.shape[0] // 2
-    tall = half // slots
-    pixel = (
-        lax.broadcasted_iota(jnp.int32, (tall, LANES), 0) * LANES
-        + lax.broadcasted_iota(jnp.int32, (tall, LANES), 1)
-    )
-    copy.wait()
-    for r in range(slots):
-        inverse = 1.0 / jnp.full((1, LANES), numbers[r], jnp.int32).astype(F32)
-        live = jnp.where(pixel < numbers[r], inverse, 0.0)
-        weight_s[r, 0] = noise_s[pl.ds(r, tall, stride=slots), :] * live
-        weight_s[r, 1] = noise_s[pl.ds(half + r, tall, stride=slots), :] * live
-
     source = lax.broadcasted_iota(jnp.int32, (2 * LANES, 1), 0)
     x, t, xx, ii = source // 128, source // 64 % 2, source // 32 % 2, source % 32
     target = (ii // 16) * 128 + (ii % 16) * 8 + x * 4 + t * 2 + xx
@@ -130,45 +121,72 @@
     order_lanes = jnp.where(
         lax.broadcasted_iota(jnp.int32, (2 * LANES, 2 * LANES), 1) == target, value, 0.0
     ).astype(BF16)
-
+    for copy in copies[:4]:
+        copy.wait()
+    numbers = [cycle_pixels[cycle_of[start + r]] for r in range(slots)]
+    for i in range(count):
+        order_s[i : i + 1, :] = jnp.full((1, LANES), orders[i], jnp.int32).astype(F32)
+    m = order_s[...]
+    at_cycle = jnp.where(
+        lax.broadcasted_iota(jnp.int32, (LANES, LANES), 0) == cycle_row[...], 1.0, 0.0
+    ).astype(BF16)
+    pick_out[...] = lax.dot_general(expand, at_cycle, NT, preferred_element_type=F32).astype(BF16)
     odd_steps = (2 * lax.broadcasted_iota(jnp.int32, (count, LANES), 1) + 1).astype(F32) * m
-    unroll = 8
+    turns, states = [], []
     for r in range(slots):
         number = jnp.full((1, LANES), numbers[r], jnp.int32).astype(F32)
         turn = turns_of(m * 32.0, number * 0.25)
         turn = turn - nearest(turn)
-        turn_cos, turn_sin = cos_turns(turn), sin_turns(turn)
+        turns.append((cos_turns(turn), sin_turns(turn)))
         base = turns_of(odd_steps, number * 2.0)
         base = base - nearest(base)
-
-        def add_pixels(chunk, state, r=r, turn_cos=turn_cos, turn_sin=turn_sin):
-            total, c, s = state
-            first = pl.multiple_of(chunk * unroll, unroll)
-            rows_q = weight_s[r, 0, pl.ds(first, unroll), :]
-            rows_u = weight_s[r, 1, pl.ds(first, unroll), :]
-            for pair in range(unroll // 2):
+        states.append((jnp.zeros((4 * count, 2 * count), F32), cos_turns(base), sin_turns(base)))
+
+    half = noise.shape[0] // 2
+    tall = half // slots
+    pixel = (
+        lax.broadcasted_iota(jnp.int32, (tall, LANES), 0) * LANES
+        + lax.broadcasted_iota(jnp.int32, (tall, LANES), 1)
+    )
+    copies[4].wait()
+    for r in range(slots):
+        inverse = 1.0 / jnp.full((1, LANES), numbers[r], jnp.int32).astype(F32)
+        live = jnp.where(pixel < numbers[r], inverse, 0.0)
+        weight_s[r, 0] = noise_s[pl.ds(r, tall, stride=slots), :] * live
+        weight_s[r, 1] = noise_s[pl.ds(half + r, tall, stride=slots), :] * live
+
+    unroll = 16
+
+    def add_pixels(chunk, states):
+        first = pl.multiple_of(chunk * unroll, unroll)
+        rows = [[weight_s[r, t, pl.ds(first, unroll), :] for t in (0, 1)] for r in range(slots)]
+        states = list(states)
+        for even in range(0, unroll, 2):
+            for r in range(slots):
+                total, c, s = states[r]
+                turn_cos, turn_sin = turns[r]
                 phases, weighted = [], []
-                for step in (2 * pair, 2 * pair + 1):
-                    q, u = rows_q[step : step + 1], rows_u[step : step + 1]
+                for step in (even, even + 1):
+                    q, u = (rows[r][t][step : step + 1] for t in (0, 1))
                     phases.append(jnp.concatenate([c, s], axis=0).astype(BF16))
                     weighted.append(jnp.concatenate([q * c, q * s, u * c, u * s], axis=0).astype(BF16))
                     c, s = c * turn_cos - s * turn_sin, s * turn_cos + c * turn_sin
                 total = total + lax.dot_general(
+                    jnp.concatenate(weighted, axis=1),
                     jnp.concatenate(phases, axis=1),
-                    jnp.concatenate(weighted, axis=1),
                     NT,
                     preferred_element_type=F32,
                 )
-            return total, c, s
-
-        total, _, _ = lax.fori_loop(
-            0,
-            tall // unroll,
-            add_pixels,
-            (jnp.zeros((2 * count, LANES), F32), cos_turns(base), sin_turns(base)),
+                states[r] = (total, c, s)
+        return tuple(states)
+
+    states = lax.fori_loop(0, tall // unroll, add_pixels, tuple(states))
+    for r in range(slots):
+        total = states[r][0]
+        rows = [total[(2 * t + x) * count : (2 * t + x + 1) * count] for x in (0, 1) for t in (0, 1)]
+        placed = lax.dot_general(
+            jnp.concatenate(rows, axis=1).astype(BF16), order_lanes, NN, preferred_element_type=F32
         )
-        pair = jnp.concatenate([total[:count], total[count:]], axis=1).astype(BF16)
-        placed = lax.dot_general(pair, order_lanes, NN, preferred_element_type=F32)
         out[:, r, :] = placed[:, :LANES]
         out[:, slots + r, :] = placed[:, LANES:]
 
@@ -243,13 +261,16 @@
             pltpu.VMEM((2 * width, cycles), BF16),
             pltpu.VMEM((comps, 4 * slots, width), F32),
         ],
-        in_specs=[SMEM, SMEM, SMEM, ANY, ANY, ANY],
+        in_specs=[ANY] * 6,
         out_specs=[VMEM] * 3,
         scratch_shapes=[
+            pltpu.SMEM(channel_of.shape, jnp.int32),
+            pltpu.SMEM(mixing.shape[::-1], F32),
+            pltpu.SMEM(m_orders.shape, jnp.int32),
             pltpu.VMEM(comp_alms.shape, F32),
             pltpu.VMEM((beam_window.shape[0], width), F32),
             pltpu.VMEM((slots * 4, 2 * width), F32),
-            pltpu.SemaphoreType.DMA((4,)),
+            pltpu.SemaphoreType.DMA((7,)),
         ],
         name="forward",
     )(channel_of, mixing.T, m_orders, comp_alms, beam_window, legendre)
@@ -260,13 +281,17 @@
     matrix, pick = pl.pallas_call(
         functools.partial(cycle_matrix_kernel, blk=blk, slots=held),
         out_shape=[pltpu.VMEM((orders, 2 * held, LANES), F32), pltpu.VMEM((2 * LANES, LANES), BF16)],
-        in_specs=[SMEM, SMEM, SMEM, VMEM, ANY],
+        in_specs=[ANY] * 5,
         out_specs=[VMEM] * 2,
         scratch_shapes=[
+            pltpu.SMEM(m_orders.shape, jnp.int32),
+            pltpu.SMEM(cycle_of.shape, jnp.int32),
+            pltpu.SMEM(cycle_pixels.shape, jnp.int32),
+            pltpu.VMEM((1, cycles), jnp.int32),
             pltpu.VMEM(noise.shape, F32),
             pltpu.VMEM((held, 2, tall, LANES), F32),
             pltpu.VMEM((orders, LANES), F32),
-            pltpu.SemaphoreType.DMA((1,)),
+            pltpu.SemaphoreType.DMA((5,)),
         ],
         name="matrices",
     )(m_orders, cycle_of, cycle_pixels, cycle_of.reshape(1, -1), noise)

time: 60.7 us -> 54.8 us (0.903)
  Pallas kernels: 13.6 us -> 7.74 us
  waiting for transfers between devices: 0.01 us -> 2.84 us
  blocking collectives: 36.6 us -> 33.8 us
    pallas_call x1, Pallas kernels: 9.79 us -> 4.63 us  [body(): pl.pallas_call(functools.partial(cycle_matrix_kernel, blk=blk, slots=held...]
    all_to_all x1, waiting for transfers between devices: 0.01 us -> 2.84 us  [move(): return lax.all_to_all(x, axis, 0, 0, tiled=True)]
    all_to_all x2, blocking collectives: 36.6 us -> 33.8 us  [move(): return lax.all_to_all(x, axis, 0, 0, tiled=True)]
    pallas_call x1, Pallas kernels: 2.45 us -> 1.8 us  [body(): pl.pallas_call(functools.partial(forward_kernel, chan=chan, blk=blk), out...]
  transfers between devices with their start and end apart: 1 -> 1, of which waited for: 0 -> 1; matrix products, arithmetic and copies ran while one was open for 0% -> 0% of each run, Pallas kernels for 16% -> 9%
where the time goes in v4:
time: 54.8 us; the launch traced here: 54.5 us
  blocking collectives  33.8 us (62%)
  starting transfers between devices  10.1 us (18%)
  Pallas kernels  7.74 us (14%)
  waiting for transfers between devices  2.84 us (5%)
    all_to_all x2, blocking collectives, move(): return lax.all_to_all(x, axis, 0, 0, tiled=True)  33.8 us
    all_to_all x1, starting transfers between devices, move(): return lax.all_to_all(x, axis, 0, 0, tiled=True)  10.1 us
    pallas_call x1, Pallas kernels, body(): pl.pallas_call(functools.partial(cycle_matrix_kernel, blk=blk, slots=held...  4.63 us
    all_to_all x1, waiting for transfers between devices, move(): return lax.all_to_all(x, axis, 0, 0, tiled=True)  2.84 us
    pallas_call x1, Pallas kernels, body(): pl.pallas_call(functools.partial(forward_kernel, chan=chan, blk=blk), out...  1.8 us
  transfers between devices with their start and end apart: 1, of which 1 were waited for; matrix products, arithmetic and copies ran while one was open for 0% of the time, Pallas kernels for 9%

profile of v4, /device:TPU:1, one launch (start us, length us, event | category | flops | bytes accessed | tf_op | source)
XLA Modules:
  0.0 54.5 jit_solution(6176576152647450536)
XLA Ops:
  0.0 1.8 %forward.1 = (f32[16,4,128]{2,1,0:T(4,128)}, bf16[512,128]{1,0:T(8,128)(2,1)S(1)}, f32[3,64,256]{2,1,0:T(8,128)S(1)}) custom-call(s32[16]{0:T(128)} %chan_of_hbm.1, f32[3,16]{1,0:T(4,128)} %bitcast.8, s32[32]{0:T(128)} %orders_hbm.3, f32[3,4,1,256]{3,2,1,0:T(1,128)} %comp.1, f32[16,4096]{1,0:T(8,128)} %beam.1, bf16[2,1,4096,128]{3,2,1,0:T(8,128)(2,1)} %legendre.1), custom_call_target="tpu_custom_call" | custom-call | tf_op jit(solution)/shard_map/forward/pallas_call | solution.py:257
  1.8 10.1 %all-to-all-start = ((f32[16,4,128]{2,1,0:T(4,128)}), f32[16,4,128]{2,1,0:T(4,128)S(1)}, u32[]{:S(2)}, u32[]{:S(2)}) async-start(f32[16,4,128]{2,1,0:T(4,128)} %get-tuple-element.10), calls=%async_computation | async-start | bytes 65536 | tf_op jit(solution)/shard_map/all_to_all | solution.py:25
  12.0 4.6 %matrices.1 = (f32[32,8,128]{2,1,0:T(8,128)S(1)}, bf16[256,128]{1,0:T(8,128)(2,1)S(1)}) custom-call(s32[32]{0:T(128)} %orders_hbm.3, s32[128]{0:T(128)} %cycle_of_hbm.1, s32[128]{0:T(128)} %cycle_pixels_hbm.1, s32[1,128]{1,0:T(1,128)} %bitcast.9, f32[512,128]{1,0:T(8,128)} %bitcast.7), custom_call_target="tpu_custom_call" | custom-call | tf_op jit(solution)/shard_map/matrices/pallas_call | solution.py:281
  16.6 2.8 %all-to-all-done.pieces = f32[16,4,128]{2,1,0:T(4,128)S(1)} async-done(((f32[16,4,128]{2,1,0:T(4,128)}), f32[16,4,128]{2,1,0:T(4,128)S(1)}, u32[]{:S(2)}, u32[]{:S(2)}) %all-to-all-start) | async-done | bytes 32800 | tf_op jit(solution)/shard_map/all_to_all | solution.py:25
  19.5 20.4 %all_to_all.15.received = bf16[32,16,128]{2,1,0:T(8,128)(2,1)S(1)} all-to-all(bf16[32,16,128]{2,1,0:T(8,128)(2,1)S(1)} %join.1), channel_id=1, replica_groups=mesh['chan'=16,'blk'=32] {'blk'}, dimensions={0} | all-to-all | bytes 262144 | tf_op jit(solution)/shard_map/all_to_all | solution.py:25
  39.9 0.5 cycles.1
  40.4 13.3 %all_to_all.16.grads = bf16[16,4,128]{2,1,0:T(4,128)(2,1)S(1)} all-to-all(bf16[16,4,128]{2,1,0:T(4,128)(2,1)S(1)} %cycles.1), channel_id=1, replica_groups=mesh['chan'=16,'blk'=32] {'chan'}, dimensions={0} | all-to-all | bytes 32768 | tf_op jit(solution)/shard_map/all_to_all | solution.py:25
  53.7 0.8 %adjoint.1 = f32[3,4,1,256]{3,2,1,0:T(1,128)} custom-call(bf16[16,4,128]{2,1,0:T(4,128)(2,1)S(1)} %all_to_all.16.grads, bf16[512,128]{1,0:T(8,128)(2,1)S(1)} %get-tuple-element.13.legendre, f32[3,64,256]{2,1,0:T(8,128)S(1)} %get-tuple-element.14.mixed), custom_call_target="tpu_custom_call" | custom-call | tf_op jit(solution)/shard_map/adjoint/pallas_call | solution.py:312
  (1 shorter events, 0.0 us)
Async XLA Ops:
  1.8 17.6 %all-to-all-start = ((f32[16,4,128]{2,1,0:T(4,128)}), f32[16,4,128]{2,1,0:T(4,128)S(1)}, u32[]{:S(2)}, u32[]{:S(2)}) async-start(f32[16,4,128]{2,1,0:T(4,128)} %get-tuple-element.10), calls=%async_computation | async-start | bytes 65536 | tf_op jit(solution)/shard_map/all_to_all | solution.py:25

commit v5 on v3

v5 whole, which is shorter than its diff:
```python
import functools

import jax
import jax.numpy as jnp
from jax import lax
from jax.experimental import pallas as pl
from jax.experimental.pallas import tpu as pltpu
from jax.sharding import PartitionSpec as P

F32 = jnp.float32
BF16 = jnp.bfloat16
LANES = 128
NT = (((1,), (1,)), ((), ()))
NN = (((1,), (0,)), ((), ()))
COS = (0.9999999887921183, -19.739204415555925, 64.93911321613162, -85.45006149635309,
       60.16698573653733, -25.965151588112157, 6.525190124026944)
SIN = (6.28318530240345, -41.341700371179485, 81.60512965170976, -76.70298335354587,
       42.02566158843437, -14.898837201069828, 3.2367039052082127)

VMEM = pl.BlockSpec(memory_space=pltpu.VMEM)
ANY = pl.BlockSpec(memory_space=pl.ANY)


def move(x, axis):
    return lax.all_to_all(x, axis, 0, 0, tiled=True)


def in_vmem(x):
    return pltpu.with_memory_space_constraint(x, pltpu.VMEM)


def nearest(x):
    return jnp.floor(x + 0.5)


def poly(z, terms):
    total = jnp.full_like(z, terms[-1])
    for term in terms[-2::-1]:
        total = total * z + term
    return total


def cos_turns(y):
    return poly(y * y, COS)


def sin_turns(y):
    return y * poly(y * y, SIN)


def turns_of(steps, period):
    inverse = 1.0 / period
    rest = steps - nearest(steps * inverse) * period
    return rest * inverse


def forward_kernel(
    chan_of_hbm, mixing_hbm, orders_hbm, cycle_of_hbm, cycle_pixels_hbm, cycle_row_hbm, comp, beam, legendre, noise,
    out, leg, mixed_out, noise_out, order_out, number_out, cycle_row_out,
    chan_of, mixing, orders, cycle_of, cycle_pixels, comp_s, beam_s, alm_s, sems, *, chan, blk, slots
):
    width = comp.shape[3]
    first = chan() * width
    copies = [
        pltpu.make_async_copy(beam.at[:, pl.ds(first, width)], beam_s, sems.at[0]),
        pltpu.make_async_copy(legendre.at[0, 0, pl.ds(first, width), :], leg.at[pl.ds(0, width)], sems.at[1]),
        pltpu.make_async_copy(legendre.at[1, 0, pl.ds(first, width), :], leg.at[pl.ds(width, width)], sems.at[2]),
        pltpu.make_async_copy(comp, comp_s, sems.at[3]),
        pltpu.make_async_copy(chan_of_hbm, chan_of, sems.at[4]),
        pltpu.make_async_copy(mixing_hbm, mixing, sems.at[5]),
        pltpu.make_async_copy(orders_hbm, orders, sems.at[6]),
        pltpu.make_async_copy(cycle_of_hbm, cycle_of, sems.at[7]),
        pltpu.make_async_copy(cycle_pixels_hbm, cycle_pixels, sems.at[8]),
        pltpu.make_async_copy(cycle_row_hbm, cycle_row_out, sems.at[9]),
        pltpu.make_async_copy(noise, noise_out, sems.at[10]),
    ]
    for n in (4, 5, 6, 3, 0, 1, 2, 7, 8, 9, 10):
        copies[n].start()
    degrees = first + lax.broadcasted_iota(jnp.int32, (1, width), 1)
    for n in (4, 5, 6, 3, 0):
        copies[n].wait()
    order = orders[blk()]
    keep = jnp.where(degrees >= order, 1.0, 0.0)
    parts = [comp_s[c, :, 0, :] for c in range(comp.shape[0])]
    for k in range(out.shape[0]):
        channel = chan_of[k]
        row = beam_s[pl.ds(channel, 1), :] * keep
        mixed = mixing[0, channel] * parts[0]
        for c in range(1, len(parts)):
            mixed = mixed + mixing[c, channel] * parts[c]
        alm = mixed * row
        twisted = jnp.concatenate([-alm[3:4], alm[2:3], alm[1:2], -alm[0:1]], axis=0)
        alm_s[4 * k : 4 * k + 4, :width] = alm
        alm_s[4 * k : 4 * k + 4, width:] = twisted
        for c in range(len(parts)):
            mixed_out[c, 4 * k : 4 * k + 4, :] = jnp.broadcast_to(mixing[c, channel] * row, (4, width))
    copies[1].wait()
    copies[2].wait()
    sums = lax.dot_general(alm_s[...].astype(BF16), leg[...], NN, preferred_element_type=F32)
    out[...] = sums.reshape(out.shape)
    for i in range(orders.shape[0]):
        order_out[i : i + 1, :] = jnp.full((1, LANES), orders[i], jnp.int32).astype(F32)
    for copy in copies[7:]:
        copy.wait()
    start = blk() * slots
    for r in range(slots):
        number_out[r : r + 1, :] = jnp.full((1, LANES), cycle_pixels[cycle_of[start + r]], jnp.int32).astype(F32)


def cycle_matrix_kernel(order_rows, numbers, cycle_row, noise, out, pick_out, weight_s):
    count = order_rows.shape[0]
    slots = out.shape[1]
    square = (LANES, LANES)
    row = lax.broadcasted_iota(jnp.int32, square, 0)
    same = jnp.where(row == lax.broadcasted_iota(jnp.int32, square, 1), 1.0, 0.0).astype(BF16)
    at_cycle = jnp.where(row == cycle_row[...], 1.0, 0.0).astype(BF16)
    pick_out[...] = lax.dot_general(same, at_cycle, NT, preferred_element_type=F32).astype(BF16)
    m = order_rows[...]
    odd_steps = (2 * lax.broadcasted_iota(jnp.int32, (count, LANES), 1) + 1).astype(F32) * m
    half = noise.shape[0] // 2
    tall = half // slots
    pixel = (
        lax.broadcasted_iota(jnp.int32, (tall, LANES), 0) * LANES
        + lax.broadcasted_iota(jnp.int32, (tall, LANES), 1)
    ).astype(F32)
    turns, states = [], []
    for r in range(slots):
        number = numbers[r : r + 1, :]
        live = jnp.where(pixel < number, 1.0 / number, 0.0)
        weight_s[r, 0] = noise[pl.ds(r, tall, stride=slots), :] * live
        weight_s[r, 1] = noise[pl.ds(half + r, tall, stride=slots), :] * live
        turn = turns_of(m * 32.0, number * 0.25)
        turn = turn - nearest(turn)
        turns.append((cos_turns(turn), sin_turns(turn)))
        base = turns_of(odd_steps, number * 2.0)
        base = base - nearest(base)
        states.append((jnp.zeros((4 * count, 2 * count), F32), cos_turns(base), sin_turns(base)))

    for even in range(0, tall, 2):
        for r in range(slots):
            total, c, s = states[r]
            turn_cos, turn_sin = turns[r]
            phases, weighted = [], []
            for step in (even, even + 1):
                q, u = (weight_s[r, t, step : step + 1, :] for t in (0, 1))
                phases.append(jnp.concatenate([c, s], axis=0).astype(BF16))
                weighted.append(jnp.concatenate([q * c, q * s, u * c, u * s], axis=0).astype(BF16))
                c, s = c * turn_cos - s * turn_sin, s * turn_cos + c * turn_sin
            total = total + lax.dot_general(
                jnp.concatenate(weighted, axis=1),
                jnp.concatenate(phases, axis=1),
                NT,
                preferred_element_type=F32,
            )
            states[r] = (total, c, s)

    source = lax.broadcasted_iota(jnp.int32, (2 * LANES, 1), 0)
    x, t, xx, ii = source // 128, source // 64 % 2, source // 32 % 2, source % 32
    target = (ii // 16) * 128 + (ii % 16) * 8 + x * 4 + t * 2 + xx
    value = jnp.where(x == xx, 1.0, -1.0)
    order_lanes = jnp.where(
        lax.broadcasted_iota(jnp.int32, (2 * LANES, 2 * LANES), 1) == target, value, 0.0
    ).astype(BF16)
    for r in range(slots):
        total = states[r][0]
        rows = [total[(2 * t + x) * count : (2 * t + x + 1) * count] for x in (0, 1) for t in (0, 1)]
        out[:, r, :] = lax.dot_general(
            jnp.concatenate(rows, axis=1).astype(BF16), order_lanes, NN, preferred_element_type=F32
        )


def join_kernel(pieces, matrix, out):
    coeffs = jnp.sum(pieces[...], axis=0)
    for i in range(out.shape[0]):
        out[i] = jnp.concatenate([matrix[i], coeffs], axis=1).astype(BF16)


def cycle_kernel(received, pick, out):
    values = received[...].astype(F32)
    coeffs = values[:, :, 2 * LANES :]
    coeffs = jnp.concatenate([coeffs, coeffs], axis=1).reshape(2 * LANES, LANES).astype(BF16)
    picks = pick[...]
    products = []
    for h in (0, 1):
        matrix = values[:, :, h * LANES : (h + 1) * LANES].reshape(LANES, LANES)
        at_slot = lax.dot_general(picks, coeffs[h * LANES : (h + 1) * LANES], NT, preferred_element_type=F32)
        products.append(matrix * at_slot)
    lane = lax.broadcasted_iota(jnp.int32, (8, 2 * LANES), 1)
    part = lane // 2 % 2 * 2 + lane // 4 % 2
    gather = jnp.where(part == lax.broadcasted_iota(jnp.int32, part.shape, 0), 1.0, 0.0).astype(BF16)

    def exact(dot, x):
        head = x.astype(BF16)
        return dot(head) + dot((x - head.astype(F32)).astype(BF16))

    by_slot = exact(
        lambda y: lax.dot_general(gather, y, NT, preferred_element_type=F32), jnp.concatenate(products, axis=1)
    )
    grads = exact(lambda y: lax.dot_general(y, picks, NN, preferred_element_type=F32), by_slot)
    out[...] = jnp.broadcast_to(grads[:4].astype(BF16)[None], out.shape)


def adjoint_kernel(grads, legendre, mixed, out):
    slots = grads.shape[0]
    width = out.shape[3]
    straight = grads[...].astype(F32).reshape(slots * 4, LANES)
    row = lax.broadcasted_iota(jnp.int32, straight.shape, 0) % 4
    up = pltpu.roll(straight, straight.shape[0] - 1, 0)
    down = pltpu.roll(straight, 1, 0)
    up3 = pltpu.roll(straight, straight.shape[0] - 3, 0)
    down3 = pltpu.roll(straight, 3, 0)
    twisted = jnp.where(row == 0, -up3, jnp.where(row == 1, up, jnp.where(row == 2, down, -down3)))
    sums = lax.dot_general(straight.astype(BF16), legendre[:width], NT, preferred_element_type=F32)
    sums = sums + lax.dot_general(twisted.astype(BF16), legendre[width:], NT, preferred_element_type=F32)
    for c in range(out.shape[0]):
        pairs = jnp.sum((sums * mixed[c]).reshape(slots // 2, 8, sums.shape[1]), axis=0)
        out[c, :, 0, :] = pairs[:4] + pairs[4:]


def body(
    comp_alms,
    legendre,
    inv_noise,
    beam_window,
    mixing,
    channel_of,
    m_orders,
    cycle_of,
    cycle_pixels,
):
    slots = channel_of.shape[0]
    orders = m_orders.shape[0]
    cycles = legendre.shape[3]
    comps, _, _, width = comp_alms.shape
    chan = functools.partial(lax.axis_index, "chan")
    blk = functools.partial(lax.axis_index, "blk")
    held = inv_noise.shape[2]
    tall = inv_noise.shape[3] // LANES
    noise = inv_noise.reshape(2, held, tall, LANES).transpose(0, 2, 1, 3).reshape(2 * tall * held, LANES)
    partial, legs, mixed, *made_of = pl.pallas_call(
        functools.partial(forward_kernel, chan=chan, blk=blk, slots=held),
        out_shape=[
            jax.ShapeDtypeStruct((slots, 4, cycles), F32),
            pltpu.VMEM((2 * width, cycles), BF16),
            pltpu.VMEM((comps, 4 * slots, width), F32),
            pltpu.VMEM(noise.shape, F32),
            pltpu.VMEM((orders, LANES), F32),
            pltpu.VMEM((held, LANES), F32),
            pltpu.VMEM((1, cycles), jnp.int32),
        ],
        in_specs=[ANY] * 10,
        out_specs=[VMEM] * 7,
        scratch_shapes=[
            pltpu.SMEM(channel_of.shape, jnp.int32),
            pltpu.SMEM(mixing.shape[::-1], F32),
            pltpu.SMEM(m_orders.shape, jnp.int32),
            pltpu.SMEM(cycle_of.shape, jnp.int32),
            pltpu.SMEM(cycle_pixels.shape, jnp.int32),
            pltpu.VMEM(comp_alms.shape, F32),
            pltpu.VMEM((beam_window.shape[0], width), F32),
            pltpu.VMEM((slots * 4, 2 * width), F32),
            pltpu.SemaphoreType.DMA((11,)),
        ],
        name="forward",
    )(
        channel_of, mixing.T, m_orders, cycle_of, cycle_pixels, cycle_of.reshape(1, -1),
        comp_alms, beam_window, legendre, noise,
    )
    pieces = move(partial, "chan")
    weights, order_rows, numbers, cycle_row = map(in_vmem, made_of)
    matrix, pick = pl.pallas_call(
        cycle_matrix_kernel,
        out_shape=[pltpu.VMEM((orders, held, 2 * LANES), F32), pltpu.VMEM((cycles, LANES), BF16)],
        in_specs=[VMEM] * 4,
        out_specs=[VMEM] * 2,
        scratch_shapes=[pltpu.VMEM((held, 2, tall, LANES), F32)],
        name="matrices",
    )(order_rows, numbers, cycle_row, weights)
    message = pl.pallas_call(
        join_kernel,
        out_shape=pltpu.VMEM((orders, held, 3 * LANES), BF16),
        in_specs=[VMEM] * 2,
        out_specs=VMEM,
        name="join",
    )(in_vmem(pieces), in_vmem(matrix))
    grads = pl.pallas_call(
        cycle_kernel,
        out_shape=pltpu.VMEM((slots, 4, cycles), BF16),
        in_specs=[VMEM] * 2,
        out_specs=VMEM,
        name="cycles",
    )(in_vmem(move(message, "blk")), in_vmem(pick))
    return pl.pallas_call(
        adjoint_kernel,
        out_shape=jax.ShapeDtypeStruct(comp_alms.shape, F32),
        in_specs=[VMEM] * 3,
        out_specs=VMEM,
        name="adjoint",
    )(in_vmem(move(grads, "chan")), in_vmem(legs), in_vmem(mixed))


def solution(mesh):
    placed = (
        P(None, None, "blk", "chan"),
        P(None, "blk", None, None),
        P("chan", None, "blk", None),
        P(),
        P(),
        P(),
        P(),
        P(),
        P(),
    )
    return jax.shard_map(
        body, mesh=mesh, in_specs=placed, out_specs=P(None, None, "blk", "chan"), check_vma=False
    )
```

time: 60.7 us -> 52.8 us (0.87)
  Pallas kernels: 13.6 us -> 6.02 us
  blocking collectives: 36.6 us -> 31.8 us
  waiting for transfers between devices: 0.01 us -> 4.55 us
    pallas_call x3, Pallas kernels: 12.3 us -> 4.75 us  [the longest x1 2.92 us: body(): pl.pallas_call(cycle_matrix_kernel, out_shape=[pltpu.VMEM((orders, held,...]
    all_to_all x2, blocking collectives: 36.6 us -> 31.8 us  [move(): return lax.all_to_all(x, axis, 0, 0, tiled=True)]
    all_to_all x1, waiting for transfers between devices: 0.01 us -> 4.55 us  [move(): return lax.all_to_all(x, axis, 0, 0, tiled=True)]
  transfers between devices with their start and end apart: 1 -> 1, of which waited for: 0 -> 1; matrix products, arithmetic and copies ran while one was open for 0% -> 0% of each run, Pallas kernels for 16% -> 6%
where the time goes in v5:
time: 52.8 us; the launch traced here: 52.5 us
  blocking collectives  31.8 us (60%)
  starting transfers between devices  10.1 us (19%)
  Pallas kernels  6.02 us (11%)
  waiting for transfers between devices  4.55 us (9%)
    all_to_all x2, blocking collectives, move(): return lax.all_to_all(x, axis, 0, 0, tiled=True)  31.8 us
    all_to_all x1, starting transfers between devices, move(): return lax.all_to_all(x, axis, 0, 0, tiled=True)  10.1 us
    all_to_all x1, waiting for transfers between devices, move(): return lax.all_to_all(x, axis, 0, 0, tiled=True)  4.55 us
    pallas_call x1, Pallas kernels, body(): pl.pallas_call(cycle_matrix_kernel, out_shape=[pltpu.VMEM((orders, held,...  2.92 us
    pallas_call x1, Pallas kernels, body(): pl.pallas_call(functools.partial(forward_kernel, chan=chan, blk=blk, slot...  1.79 us
  transfers between devices with their start and end apart: 1, of which 1 were waited for; matrix products, arithmetic and copies ran while one was open for 0% of the time, Pallas kernels for 6%

profile of v5, /device:TPU:1, one launch (start us, length us, event | category | flops | bytes accessed | tf_op | source)
XLA Modules:
  0.0 52.5 jit_solution(8398795368414835700)
XLA Ops:
  0.0 1.8 %forward.1 = (f32[16,4,128]{2,1,0:T(4,128)}, bf16[512,128]{1,0:T(8,128)(2,1)S(1)}, f32[3,64,256]{2,1,0:T(8,128)S(1)}, f32[512,128]{1,0:T(8,128)S(1)}, f32[32,128...) custom-call(s32[16]{0:T(128)} %chan_of_hbm.1, f32[3,16]{1,0:T(4,128)} %bitcast.8, s32[32]{0:T(128)} %orders_hbm.1, ...), custom_call_target="tpu_custom_call" | custom-call | tf_op jit(solution)/shard_map/forward/pallas_call | solution.py:240
  1.8 10.1 %all-to-all-start = ((f32[16,4,128]{2,1,0:T(4,128)}), f32[16,4,128]{2,1,0:T(4,128)S(1)}, u32[]{:S(2)}, u32[]{:S(2)}) async-start(f32[16,4,128]{2,1,0:T(4,128)} %get-tuple-element.14), calls=%async_computation | async-start | bytes 65536 | tf_op jit(solution)/shard_map/all_to_all | solution.py:25
  12.0 2.9 %matrices.1 = (f32[32,4,256]{2,1,0:T(4,128)S(1)}, bf16[128,128]{1,0:T(8,128)(2,1)S(1)}) custom-call(f32[32,128]{1,0:T(8,128)S(1)} %get-tuple-element.15.order_rows, f32[4,128]{1,0:T(4,128)S(1)} %get-tuple-element.16.numbers, s32[1,128]{1,0:T(1,128)S(1)} %get-tuple-element.17.cycle_row, f32[512,128]{1,0:T(8,128)S(1)} %get-tuple-element.18.noise), custom_call_target="tpu_custom_call" | custom-call | tf_op jit(solution)/shard_map/matrices/pallas_call | solution.py:271
  14.9 4.5 %all-to-all-done.pieces = f32[16,4,128]{2,1,0:T(4,128)S(1)} async-done(((f32[16,4,128]{2,1,0:T(4,128)}), f32[16,4,128]{2,1,0:T(4,128)S(1)}, u32[]{:S(2)}, u32[]{:S(2)}) %all-to-all-start) | async-done | bytes 32800 | tf_op jit(solution)/shard_map/all_to_all | solution.py:25
  19.5 20.2 %all_to_all.15.received = bf16[32,4,384]{2,1,0:T(4,128)(2,1)S(1)} all-to-all(bf16[32,4,384]{2,1,0:T(4,128)(2,1)S(1)} %join.1), channel_id=1, replica_groups=mesh['chan'=16,'blk'=32] {'blk'}, dimensions={0} | all-to-all | bytes 196608 | tf_op jit(solution)/shard_map/all_to_all | solution.py:25
  39.6 0.5 cycles.1
  40.1 11.6 %all_to_all.16.grads = bf16[16,4,128]{2,1,0:T(4,128)(2,1)S(1)} all-to-all(bf16[16,4,128]{2,1,0:T(4,128)(2,1)S(1)} %cycles.1), channel_id=1, replica_groups=mesh['chan'=16,'blk'=32] {'chan'}, dimensions={0} | all-to-all | bytes 32768 | tf_op jit(solution)/shard_map/all_to_all | solution.py:25
  51.7 0.8 %adjoint.1 = f32[3,4,1,256]{3,2,1,0:T(1,128)} custom-call(bf16[16,4,128]{2,1,0:T(4,128)(2,1)S(1)} %all_to_all.16.grads, bf16[512,128]{1,0:T(8,128)(2,1)S(1)} %get-tuple-element.21.legendre, f32[3,64,256]{2,1,0:T(8,128)S(1)} %get-tuple-element.22.mixed), custom_call_target="tpu_custom_call" | custom-call | tf_op jit(solution)/shard_map/adjoint/pallas_call | solution.py:293
  (1 shorter events, 0.0 us)
Async XLA Ops:
  1.8 17.6 %all-to-all-start = ((f32[16,4,128]{2,1,0:T(4,128)}), f32[16,4,128]{2,1,0:T(4,128)S(1)}, u32[]{:S(2)}, u32[]{:S(2)}) async-start(f32[16,4,128]{2,1,0:T(4,128)} %get-tuple-element.14), calls=%async_computation | async-start | bytes 65536 | tf_op jit(solution)/shard_map/all_to_all | solution.py:25

commit v6 on v5

--- a/solution.py
+++ b/solution.py
@@ -21,8 +21,12 @@
 ANY = pl.BlockSpec(memory_space=pl.ANY)
 
 
+FLIP = {"chan": 8, "blk": 18}
+
+
 def move(x, axis):
-    return lax.all_to_all(x, axis, 0, 0, tiled=True)
+    members = [j ^ FLIP[axis] for j in range(x.shape[0])]
+    return lax.all_to_all(x, axis, 0, 0, tiled=True, axis_index_groups=[members])
 
 
 def in_vmem(x):
@@ -83,7 +87,7 @@
     keep = jnp.where(degrees >= order, 1.0, 0.0)
     parts = [comp_s[c, :, 0, :] for c in range(comp.shape[0])]
     for k in range(out.shape[0]):
-        channel = chan_of[k]
+        channel = chan_of[k ^ FLIP["chan"]]
         row = beam_s[pl.ds(channel, 1), :] * keep
         mixed = mixing[0, channel] * parts[0]
         for c in range(1, len(parts)):
@@ -112,7 +116,7 @@
     slots = out.shape[1]
     square = (LANES, LANES)
     row = lax.broadcasted_iota(jnp.int32, square, 0)
-    same = jnp.where(row == lax.broadcasted_iota(jnp.int32, square, 1), 1.0, 0.0).astype(BF16)
+    same = jnp.where(row == lax.broadcasted_iota(jnp.int32, square, 1) ^ (slots * FLIP["blk"]), 1.0, 0.0).astype(BF16)
     at_cycle = jnp.where(row == cycle_row[...], 1.0, 0.0).astype(BF16)
     pick_out[...] = lax.dot_general(same, at_cycle, NT, preferred_element_type=F32).astype(BF16)
     m = order_rows[...]
@@ -155,7 +159,7 @@
             states[r] = (total, c, s)
 
     source = lax.broadcasted_iota(jnp.int32, (2 * LANES, 1), 0)
-    x, t, xx, ii = source // 128, source // 64 % 2, source // 32 % 2, source % 32
+    x, t, xx, ii = source // 128, source // 64 % 2, source // 32 % 2, source % 32 ^ FLIP["blk"]
     target = (ii // 16) * 128 + (ii % 16) * 8 + x * 4 + t * 2 + xx
     value = jnp.where(x == xx, 1.0, -1.0)
     order_lanes = jnp.where(
@@ -172,7 +176,7 @@
 def join_kernel(pieces, matrix, out):
     coeffs = jnp.sum(pieces[...], axis=0)
     for i in range(out.shape[0]):
-        out[i] = jnp.concatenate([matrix[i], coeffs], axis=1).astype(BF16)
+        out[i] = jnp.concatenate([matrix[i ^ FLIP["blk"]], coeffs], axis=1).astype(BF16)
 
 
 def cycle_kernel(received, pick, out):

time: 52.8 us -> 46.1 us (0.87)
  blocking collectives: 31.8 us -> 26 us
  waiting for transfers between devices: 4.55 us -> 0.01 us
  starting transfers between devices: 10.1 us -> 13.8 us
    all_to_all x2, blocking collectives: 31.8 us -> 26 us  [move(): lax.all_to_all(x, axis, 0, 0, tiled=True, axis_index_groups=[members])]
    all_to_all x1, waiting for transfers between devices: 4.55 us -> 0.01 us  [move(): lax.all_to_all(x, axis, 0, 0, tiled=True, axis_index_groups=[members])]
    all_to_all x1, starting transfers between devices: 10.1 us -> 13.8 us  [move(): lax.all_to_all(x, axis, 0, 0, tiled=True, axis_index_groups=[members])]
  transfers between devices with their start and end apart: 1 -> 1, of which waited for: 1 -> 0; matrix products, arithmetic and copies ran while one was open for 0% -> 0% of each run, Pallas kernels for 6% -> 6%
where the time goes in v6:
time: 46.1 us; the launch traced here: 45.9 us
  blocking collectives  26 us (56%)
  starting transfers between devices  13.8 us (30%)
  Pallas kernels  6.04 us (13%)
    all_to_all x2, blocking collectives, move(): lax.all_to_all(x, axis, 0, 0, tiled=True, axis_index_groups=[members])  26 us
    all_to_all x1, starting transfers between devices, move(): lax.all_to_all(x, axis, 0, 0, tiled=True, axis_index_groups=[members])  13.8 us
    pallas_call x1, Pallas kernels, body(): pl.pallas_call(cycle_matrix_kernel, out_shape=[pltpu.VMEM((orders, held,...  2.94 us
    pallas_call x1, Pallas kernels, body(): pl.pallas_call(functools.partial(forward_kernel, chan=chan, blk=blk, slot...  1.79 us
  transfers between devices with their start and end apart: 1, of which 0 were waited for; matrix products, arithmetic and copies ran while one was open for 0% of the time, Pallas kernels for 6%

profile of v6, /device:TPU:1, one launch (start us, length us, event | category | flops | bytes accessed | tf_op | source)
XLA Modules:
  0.0 45.9 jit_solution(18445620532932598298)
XLA Ops:
  0.0 1.8 %forward.1 = (f32[16,4,128]{2,1,0:T(4,128)}, bf16[512,128]{1,0:T(8,128)(2,1)S(1)}, f32[3,64,256]{2,1,0:T(8,128)S(1)}, f32[512,128]{1,0:T(8,128)S(1)}, f32[32,128...) custom-call(s32[16]{0:T(128)} %chan_of_hbm.1, f32[3,16]{1,0:T(4,128)} %bitcast.8, s32[32]{0:T(128)} %orders_hbm.1, ...), custom_call_target="tpu_custom_call" | custom-call | tf_op jit(solution)/shard_map/forward/pallas_call | solution.py:244
  1.8 13.8 %all-to-all-start = ((f32[16,4,128]{2,1,0:T(4,128)}), f32[16,4,128]{2,1,0:T(4,128)S(1)}, u32[]{:S(2)}, u32[]{:S(2)}) async-start(f32[16,4,128]{2,1,0:T(4,128)} %get-tuple-element.14), calls=%async_computation | async-start | bytes 65536 | tf_op jit(solution)/shard_map/all_to_all | solution.py:29
  15.6 2.9 %matrices.1 = (f32[32,4,256]{2,1,0:T(4,128)S(1)}, bf16[128,128]{1,0:T(8,128)(2,1)S(1)}) custom-call(f32[32,128]{1,0:T(8,128)S(1)} %get-tuple-element.15.order_rows, f32[4,128]{1,0:T(4,128)S(1)} %get-tuple-element.16.numbers, s32[1,128]{1,0:T(1,128)S(1)} %get-tuple-element.17.cycle_row, f32[512,128]{1,0:T(8,128)S(1)} %get-tuple-element.18.noise), custom_call_target="tpu_custom_call" | custom-call | tf_op jit(solution)/shard_map/matrices/pallas_call | solution.py:275
  18.5 0.0 all-to-all-done.pieces
  18.6 15.2 %all_to_all.15.received = bf16[32,4,384]{2,1,0:T(4,128)(2,1)S(1)} all-to-all(bf16[32,4,384]{2,1,0:T(4,128)(2,1)S(1)} %join.1), channel_id=1, replica_groups={{18,19,16,17,22,23,20,21,26,27,24,25,30,31,28,29,2,3,0,1,6,7,4,5,10,11,..., dimensions={0} | all-to-all | bytes 196608 | tf_op jit(solution)/shard_map/all_to_all | solution.py:29
  33.8 0.5 %cycles.1 = bf16[16,4,128]{2,1,0:T(4,128)(2,1)S(1)} custom-call(bf16[32,4,384]{2,1,0:T(4,128)(2,1)S(1)} %all_to_all.15.received, bf16[128,128]{1,0:T(8,128)(2,1)S(1)} %get-tuple-element.20.pick), custom_call_target="tpu_custom_call" | custom-call | tf_op jit(solution)/shard_map/cycles/pallas_call | solution.py:290
  34.2 10.8 %all_to_all.16.grads = bf16[16,4,128]{2,1,0:T(4,128)(2,1)S(1)} all-to-all(bf16[16,4,128]{2,1,0:T(4,128)(2,1)S(1)} %cycles.1), channel_id=1, replica_groups={{256,288,320,352,384,416,448,480,0,32,64,96,128,160,192,224},{257,289,3..., dimensions={0} | all-to-all | bytes 32768 | tf_op jit(solution)/shard_map/all_to_all | solution.py:29
  45.1 0.8 %adjoint.1 = f32[3,4,1,256]{3,2,1,0:T(1,128)} custom-call(bf16[16,4,128]{2,1,0:T(4,128)(2,1)S(1)} %all_to_all.16.grads, bf16[512,128]{1,0:T(8,128)(2,1)S(1)} %get-tuple-element.21.legendre, f32[3,64,256]{2,1,0:T(8,128)S(1)} %get-tuple-element.22.mixed), custom_call_target="tpu_custom_call" | custom-call | tf_op jit(solution)/shard_map/adjoint/pallas_call | solution.py:297
  (1 shorter events, 0.0 us)
Async XLA Ops:
  1.8 16.7 %all-to-all-start = ((f32[16,4,128]{2,1,0:T(4,128)}), f32[16,4,128]{2,1,0:T(4,128)S(1)}, u32[]{:S(2)}, u32[]{:S(2)}) async-start(f32[16,4,128]{2,1,0:T(4,128)} %get-tuple-element.14), calls=%async_computation | async-start | bytes 65536 | tf_op jit(solution)/shard_map/all_to_all | solution.py:29

commit v7 on v6

--- a/solution.py
+++ b/solution.py
@@ -21,11 +21,11 @@
 ANY = pl.BlockSpec(memory_space=pl.ANY)
 
 
-FLIP = {"chan": 8, "blk": 18}
-
-
-def move(x, axis):
-    members = [j ^ FLIP[axis] for j in range(x.shape[0])]
+FLIP = {"out": 11, "blk": 26, "home": 9}
+
+
+def move(x, axis, leg):
+    members = [j ^ FLIP[leg] for j in range(x.shape[0])]
     return lax.all_to_all(x, axis, 0, 0, tiled=True, axis_index_groups=[members])
 
 
@@ -87,7 +87,7 @@
     keep = jnp.where(degrees >= order, 1.0, 0.0)
     parts = [comp_s[c, :, 0, :] for c in range(comp.shape[0])]
     for k in range(out.shape[0]):
-        channel = chan_of[k ^ FLIP["chan"]]
+        channel = chan_of[k ^ FLIP["out"]]
         row = beam_s[pl.ds(channel, 1), :] * keep
         mixed = mixing[0, channel] * parts[0]
         for c in range(1, len(parts)):
@@ -96,8 +96,9 @@
         twisted = jnp.concatenate([-alm[3:4], alm[2:3], alm[1:2], -alm[0:1]], axis=0)
         alm_s[4 * k : 4 * k + 4, :width] = alm
         alm_s[4 * k : 4 * k + 4, width:] = twisted
+        place = k ^ FLIP["out"] ^ FLIP["home"]
         for c in range(len(parts)):
-            mixed_out[c, 4 * k : 4 * k + 4, :] = jnp.broadcast_to(mixing[c, channel] * row, (4, width))
+            mixed_out[c, 4 * place : 4 * place + 4, :] = jnp.broadcast_to(mixing[c, channel] * row, (4, width))
     copies[1].wait()
     copies[2].wait()
     sums = lax.dot_general(alm_s[...].astype(BF16), leg[...], NN, preferred_element_type=F32)
@@ -270,7 +271,7 @@
         channel_of, mixing.T, m_orders, cycle_of, cycle_pixels, cycle_of.reshape(1, -1),
         comp_alms, beam_window, legendre, noise,
     )
-    pieces = move(partial, "chan")
+    pieces = move(partial, "chan", "out")
     weights, order_rows, numbers, cycle_row = map(in_vmem, made_of)
     matrix, pick = pl.pallas_call(
         cycle_matrix_kernel,
@@ -293,14 +294,14 @@
         in_specs=[VMEM] * 2,
         out_specs=VMEM,
         name="cycles",
-    )(in_vmem(move(message, "blk")), in_vmem(pick))
+    )(in_vmem(move(message, "blk", "blk")), in_vmem(pick))
     return pl.pallas_call(
         adjoint_kernel,
         out_shape=jax.ShapeDtypeStruct(comp_alms.shape, F32),
         in_specs=[VMEM] * 3,
         out_specs=VMEM,
         name="adjoint",
-    )(in_vmem(move(grads, "chan")), in_vmem(legs), in_vmem(mixed))
+    )(in_vmem(move(grads, "chan", "home")), in_vmem(legs), in_vmem(mixed))
 
 
 def solution(mesh):

time: 46.1 us -> 44.7 us (0.970)
  starting transfers between devices: 13.8 us -> 12.5 us
  blocking collectives: 26 us -> 25.4 us
    all_to_all x1, starting transfers between devices: 13.8 us -> 12.5 us  [move(): lax.all_to_all(x, axis, 0, 0, tiled=True, axis_index_groups=[members])]
    all_to_all x2, blocking collectives: 26 us -> 25.4 us  [move(): lax.all_to_all(x, axis, 0, 0, tiled=True, axis_index_groups=[members])]
  transfers between devices with their start and end apart: 1 -> 1, of which waited for: 0 -> 1; matrix products, arithmetic and copies ran while one was open for 0% -> 0% of each run, Pallas kernels for 6% -> 7%
where the time goes in v7:
time: 44.7 us; the launch traced here: 44.5 us
  blocking collectives  25.4 us (57%)
  starting transfers between devices  12.5 us (28%)
  Pallas kernels  6.04 us (14%)
  waiting for transfers between devices  0.46 us (1%)
    all_to_all x2, blocking collectives, move(): lax.all_to_all(x, axis, 0, 0, tiled=True, axis_index_groups=[members])  25.4 us
    all_to_all x1, starting transfers between devices, move(): lax.all_to_all(x, axis, 0, 0, tiled=True, axis_index_groups=[members])  12.5 us
    pallas_call x1, Pallas kernels, body(): pl.pallas_call(cycle_matrix_kernel, out_shape=[pltpu.VMEM((orders, held,...  2.94 us
    pallas_call x1, Pallas kernels, body(): pl.pallas_call(functools.partial(forward_kernel, chan=chan, blk=blk, slot...  1.79 us
  transfers between devices with their start and end apart: 1, of which 1 were waited for; matrix products, arithmetic and copies ran while one was open for 0% of the time, Pallas kernels for 7%

profile of v7, /device:TPU:1, one launch (start us, length us, event | category | flops | bytes accessed | tf_op | source)
XLA Modules:
  0.0 44.5 jit_solution(16556776258276215414)
XLA Ops:
  0.0 1.8 %forward.1 = (f32[16,4,128]{2,1,0:T(4,128)}, bf16[512,128]{1,0:T(8,128)(2,1)S(1)}, f32[3,64,256]{2,1,0:T(8,128)S(1)}, f32[512,128]{1,0:T(8,128)S(1)}, f32[32,128...) custom-call(s32[16]{0:T(128)} %chan_of_hbm.1, f32[3,16]{1,0:T(4,128)} %bitcast.8, s32[32]{0:T(128)} %orders_hbm.1, ...), custom_call_target="tpu_custom_call" | custom-call | tf_op jit(solution)/shard_map/forward/pallas_call | solution.py:245
  1.8 12.5 %all-to-all-start = ((f32[16,4,128]{2,1,0:T(4,128)}), f32[16,4,128]{2,1,0:T(4,128)S(1)}, u32[]{:S(2)}, u32[]{:S(2)}) async-start(f32[16,4,128]{2,1,0:T(4,128)} %get-tuple-element.14), calls=%async_computation | async-start | bytes 65536 | tf_op jit(solution)/shard_map/all_to_all | solution.py:29
  14.3 2.9 %matrices.1 = (f32[32,4,256]{2,1,0:T(4,128)S(1)}, bf16[128,128]{1,0:T(8,128)(2,1)S(1)}) custom-call(f32[32,128]{1,0:T(8,128)S(1)} %get-tuple-element.15.order_rows, f32[4,128]{1,0:T(4,128)S(1)} %get-tuple-element.16.numbers, s32[1,128]{1,0:T(1,128)S(1)} %get-tuple-element.17.cycle_row, f32[512,128]{1,0:T(8,128)S(1)} %get-tuple-element.18.noise), custom_call_target="tpu_custom_call" | custom-call | tf_op jit(solution)/shard_map/matrices/pallas_call | solution.py:276
  17.3 0.5 %all-to-all-done.pieces = f32[16,4,128]{2,1,0:T(4,128)S(1)} async-done(((f32[16,4,128]{2,1,0:T(4,128)}), f32[16,4,128]{2,1,0:T(4,128)S(1)}, u32[]{:S(2)}, u32[]{:S(2)}) %all-to-all-start) | async-done | bytes 32800 | tf_op jit(solution)/shard_map/all_to_all | solution.py:29
  17.8 15.0 %all_to_all.15.received = bf16[32,4,384]{2,1,0:T(4,128)(2,1)S(1)} all-to-all(bf16[32,4,384]{2,1,0:T(4,128)(2,1)S(1)} %join.1), channel_id=1, replica_groups={{26,27,24,25,30,31,28,29,18,19,16,17,22,23,20,21,10,11,8,9,14,15,12,13,..., dimensions={0} | all-to-all | bytes 196608 | tf_op jit(solution)/shard_map/all_to_all | solution.py:29
  32.8 0.5 %cycles.1 = bf16[16,4,128]{2,1,0:T(4,128)(2,1)S(1)} custom-call(bf16[32,4,384]{2,1,0:T(4,128)(2,1)S(1)} %all_to_all.15.received, bf16[128,128]{1,0:T(8,128)(2,1)S(1)} %get-tuple-element.20.pick), custom_call_target="tpu_custom_call" | custom-call | tf_op jit(solution)/shard_map/cycles/pallas_call | solution.py:291
  33.3 10.4 %all_to_all.16.grads = bf16[16,4,128]{2,1,0:T(4,128)(2,1)S(1)} all-to-all(bf16[16,4,128]{2,1,0:T(4,128)(2,1)S(1)} %cycles.1), channel_id=1, replica_groups={{288,256,352,320,416,384,480,448,32,0,96,64,160,128,224,192},{289,257,3..., dimensions={0} | all-to-all | bytes 32768 | tf_op jit(solution)/shard_map/all_to_all | solution.py:29
  43.7 0.8 %adjoint.1 = f32[3,4,1,256]{3,2,1,0:T(1,128)} custom-call(bf16[16,4,128]{2,1,0:T(4,128)(2,1)S(1)} %all_to_all.16.grads, bf16[512,128]{1,0:T(8,128)(2,1)S(1)} %get-tuple-element.21.legendre, f32[3,64,256]{2,1,0:T(8,128)S(1)} %get-tuple-element.22.mixed), custom_call_target="tpu_custom_call" | custom-call | tf_op jit(solution)/shard_map/adjoint/pallas_call | solution.py:298
  (1 shorter events, 0.0 us)
Async XLA Ops:
  1.8 16.0 %all-to-all-start = ((f32[16,4,128]{2,1,0:T(4,128)}), f32[16,4,128]{2,1,0:T(4,128)S(1)}, u32[]{:S(2)}, u32[]{:S(2)}) async-start(f32[16,4,128]{2,1,0:T(4,128)} %get-tuple-element.14), calls=%async_computation | async-start | bytes 65536 | tf_op jit(solution)/shard_map/all_to_all | solution.py:29

commit v8 on v7

--- a/solution.py
+++ b/solution.py
@@ -215,8 +215,12 @@
     up3 = pltpu.roll(straight, straight.shape[0] - 3, 0)
     down3 = pltpu.roll(straight, 3, 0)
     twisted = jnp.where(row == 0, -up3, jnp.where(row == 1, up, jnp.where(row == 2, down, -down3)))
-    sums = lax.dot_general(straight.astype(BF16), legendre[:width], NT, preferred_element_type=F32)
-    sums = sums + lax.dot_general(twisted.astype(BF16), legendre[width:], NT, preferred_element_type=F32)
+    sums = lax.dot_general(
+        jnp.concatenate([straight, twisted], axis=1).astype(BF16),
+        jnp.concatenate([legendre[:width], legendre[width:]], axis=1),
+        NT,
+        preferred_element_type=F32,
+    )
     for c in range(out.shape[0]):
         pairs = jnp.sum((sums * mixed[c]).reshape(slots // 2, 8, sums.shape[1]), axis=0)
         out[c, :, 0, :] = pairs[:4] + pairs[4:]

time: 44.7 us -> 44.7 us (level)
  no operation moved by 1% of the time
where the time goes in v8:
time: 44.7 us; the launch traced here: 44.5 us
  blocking collectives  25.4 us (57%)
  starting transfers between devices  12.5 us (28%)
  Pallas kernels  6.05 us (14%)
  waiting for transfers between devices  0.46 us (1%)
    all_to_all x2, blocking collectives, move(): lax.all_to_all(x, axis, 0, 0, tiled=True, axis_index_groups=[members])  25.4 us
    all_to_all x1, starting transfers between devices, move(): lax.all_to_all(x, axis, 0, 0, tiled=True, axis_index_groups=[members])  12.5 us
    pallas_call x1, Pallas kernels, body(): pl.pallas_call(cycle_matrix_kernel, out_shape=[pltpu.VMEM((orders, held,...  2.94 us
    pallas_call x1, Pallas kernels, body(): pl.pallas_call(functools.partial(forward_kernel, chan=chan, blk=blk, slot...  1.79 us
  transfers between devices with their start and end apart: 1, of which 1 were waited for; matrix products, arithmetic and copies ran while one was open for 0% of the time, Pallas kernels for 7%

profile of v8, /device:TPU:1, one launch (start us, length us, event | category | flops | bytes accessed | tf_op | source)
XLA Modules:
  0.0 44.5 jit_solution(4687618920244849784)
XLA Ops:
  0.0 1.8 %forward.1 = (f32[16,4,128]{2,1,0:T(4,128)}, bf16[512,128]{1,0:T(8,128)(2,1)S(1)}, f32[3,64,256]{2,1,0:T(8,128)S(1)}, f32[512,128]{1,0:T(8,128)S(1)}, f32[32,128...) custom-call(s32[16]{0:T(128)} %chan_of_hbm.1, f32[3,16]{1,0:T(4,128)} %bitcast.8, s32[32]{0:T(128)} %orders_hbm.1, ...), custom_call_target="tpu_custom_call" | custom-call | tf_op jit(solution)/shard_map/forward/pallas_call | solution.py:249
  1.8 12.5 %all-to-all-start = ((f32[16,4,128]{2,1,0:T(4,128)}), f32[16,4,128]{2,1,0:T(4,128)S(1)}, u32[]{:S(2)}, u32[]{:S(2)}) async-start(f32[16,4,128]{2,1,0:T(4,128)} %get-tuple-element.14), calls=%async_computation | async-start | bytes 65536 | tf_op jit(solution)/shard_map/all_to_all | solution.py:29
  14.3 2.9 %matrices.1 = (f32[32,4,256]{2,1,0:T(4,128)S(1)}, bf16[128,128]{1,0:T(8,128)(2,1)S(1)}) custom-call(f32[32,128]{1,0:T(8,128)S(1)} %get-tuple-element.15.order_rows, f32[4,128]{1,0:T(4,128)S(1)} %get-tuple-element.16.numbers, s32[1,128]{1,0:T(1,128)S(1)} %get-tuple-element.17.cycle_row, f32[512,128]{1,0:T(8,128)S(1)} %get-tuple-element.18.noise), custom_call_target="tpu_custom_call" | custom-call | tf_op jit(solution)/shard_map/matrices/pallas_call | solution.py:280
  17.3 0.5 %all-to-all-done.pieces = f32[16,4,128]{2,1,0:T(4,128)S(1)} async-done(((f32[16,4,128]{2,1,0:T(4,128)}), f32[16,4,128]{2,1,0:T(4,128)S(1)}, u32[]{:S(2)}, u32[]{:S(2)}) %all-to-all-start) | async-done | bytes 32800 | tf_op jit(solution)/shard_map/all_to_all | solution.py:29
  17.8 15.0 %all_to_all.15.received = bf16[32,4,384]{2,1,0:T(4,128)(2,1)S(1)} all-to-all(bf16[32,4,384]{2,1,0:T(4,128)(2,1)S(1)} %join.1), channel_id=1, replica_groups={{26,27,24,25,30,31,28,29,18,19,16,17,22,23,20,21,10,11,8,9,14,15,12,13,..., dimensions={0} | all-to-all | bytes 196608 | tf_op jit(solution)/shard_map/all_to_all | solution.py:29
  32.8 0.5 %cycles.1 = bf16[16,4,128]{2,1,0:T(4,128)(2,1)S(1)} custom-call(bf16[32,4,384]{2,1,0:T(4,128)(2,1)S(1)} %all_to_all.15.received, bf16[128,128]{1,0:T(8,128)(2,1)S(1)} %get-tuple-element.20.pick), custom_call_target="tpu_custom_call" | custom-call | tf_op jit(solution)/shard_map/cycles/pallas_call | solution.py:295
  33.3 10.4 %all_to_all.16.grads = bf16[16,4,128]{2,1,0:T(4,128)(2,1)S(1)} all-to-all(bf16[16,4,128]{2,1,0:T(4,128)(2,1)S(1)} %cycles.1), channel_id=1, replica_groups={{288,256,352,320,416,384,480,448,32,0,96,64,160,128,224,192},{289,257,3..., dimensions={0} | all-to-all | bytes 32768 | tf_op jit(solution)/shard_map/all_to_all | solution.py:29
  43.7 0.8 %adjoint.1 = f32[3,4,1,256]{3,2,1,0:T(1,128)} custom-call(bf16[16,4,128]{2,1,0:T(4,128)(2,1)S(1)} %all_to_all.16.grads, bf16[512,128]{1,0:T(8,128)(2,1)S(1)} %get-tuple-element.21.legendre, f32[3,64,256]{2,1,0:T(8,128)S(1)} %get-tuple-element.22.mixed), custom_call_target="tpu_custom_call" | custom-call | tf_op jit(solution)/shard_map/adjoint/pallas_call | solution.py:302
  (1 shorter events, 0.0 us)
Async XLA Ops:
  1.8 16.0 %all-to-all-start = ((f32[16,4,128]{2,1,0:T(4,128)}), f32[16,4,128]{2,1,0:T(4,128)S(1)}, u32[]{:S(2)}, u32[]{:S(2)}) async-start(f32[16,4,128]{2,1,0:T(4,128)} %get-tuple-element.14), calls=%async_computation | async-start | bytes 65536 | tf_op jit(solution)/shard_map/all_to_all | solution.py:29

commit v9 on v8

--- a/solution.py
+++ b/solution.py
@@ -201,7 +201,10 @@
     by_slot = exact(
         lambda y: lax.dot_general(gather, y, NT, preferred_element_type=F32), jnp.concatenate(products, axis=1)
     )
-    grads = exact(lambda y: lax.dot_general(y, picks, NN, preferred_element_type=F32), by_slot)
+    head = by_slot.astype(BF16).astype(F32)
+    halves = jnp.concatenate([head, by_slot - head], axis=0).astype(BF16)
+    halves = lax.dot_general(halves, picks, NN, preferred_element_type=F32)
+    grads = halves[:8] + halves[8:]
     out[...] = jnp.broadcast_to(grads[:4].astype(BF16)[None], out.shape)
 
 

time: 44.7 us -> 44.8 us (level)
  no operation moved by 1% of the time
where the time goes in v9:
time: 44.8 us; the launch traced here: 44.5 us
  blocking collectives  25.5 us (57%)
  starting transfers between devices  12.5 us (28%)
  Pallas kernels  6.04 us (13%)
  waiting for transfers between devices  0.46 us (1%)
    all_to_all x2, blocking collectives, move(): lax.all_to_all(x, axis, 0, 0, tiled=True, axis_index_groups=[members])  25.5 us
    all_to_all x1, starting transfers between devices, move(): lax.all_to_all(x, axis, 0, 0, tiled=True, axis_index_groups=[members])  12.5 us
    pallas_call x1, Pallas kernels, body(): pl.pallas_call(cycle_matrix_kernel, out_shape=[pltpu.VMEM((orders, held,...  2.94 us
    pallas_call x1, Pallas kernels, body(): pl.pallas_call(functools.partial(forward_kernel, chan=chan, blk=blk, slot...  1.79 us
  transfers between devices with their start and end apart: 1, of which 1 were waited for; matrix products, arithmetic and copies ran while one was open for 0% of the time, Pallas kernels for 7%

profile of v9, /device:TPU:1, one launch (start us, length us, event | category | flops | bytes accessed | tf_op | source)
XLA Modules:
  0.0 44.5 jit_solution(416552052610272602)
XLA Ops:
  0.0 1.8 %forward.1 = (f32[16,4,128]{2,1,0:T(4,128)}, bf16[512,128]{1,0:T(8,128)(2,1)S(1)}, f32[3,64,256]{2,1,0:T(8,128)S(1)}, f32[512,128]{1,0:T(8,128)S(1)}, f32[32,128...) custom-call(s32[16]{0:T(128)} %chan_of_hbm.1, f32[3,16]{1,0:T(4,128)} %bitcast.8, s32[32]{0:T(128)} %orders_hbm.1, ...), custom_call_target="tpu_custom_call" | custom-call | tf_op jit(solution)/shard_map/forward/pallas_call | solution.py:252
  1.8 12.5 %all-to-all-start = ((f32[16,4,128]{2,1,0:T(4,128)}), f32[16,4,128]{2,1,0:T(4,128)S(1)}, u32[]{:S(2)}, u32[]{:S(2)}) async-start(f32[16,4,128]{2,1,0:T(4,128)} %get-tuple-element.14), calls=%async_computation | async-start | bytes 65536 | tf_op jit(solution)/shard_map/all_to_all | solution.py:29
  14.3 2.9 %matrices.1 = (f32[32,4,256]{2,1,0:T(4,128)S(1)}, bf16[128,128]{1,0:T(8,128)(2,1)S(1)}) custom-call(f32[32,128]{1,0:T(8,128)S(1)} %get-tuple-element.15.order_rows, f32[4,128]{1,0:T(4,128)S(1)} %get-tuple-element.16.numbers, s32[1,128]{1,0:T(1,128)S(1)} %get-tuple-element.17.cycle_row, f32[512,128]{1,0:T(8,128)S(1)} %get-tuple-element.18.noise), custom_call_target="tpu_custom_call" | custom-call | tf_op jit(solution)/shard_map/matrices/pallas_call | solution.py:283
  17.3 0.5 %all-to-all-done.pieces = f32[16,4,128]{2,1,0:T(4,128)S(1)} async-done(((f32[16,4,128]{2,1,0:T(4,128)}), f32[16,4,128]{2,1,0:T(4,128)S(1)}, u32[]{:S(2)}, u32[]{:S(2)}) %all-to-all-start) | async-done | bytes 32800 | tf_op jit(solution)/shard_map/all_to_all | solution.py:29
  17.8 15.0 %all_to_all.15.received = bf16[32,4,384]{2,1,0:T(4,128)(2,1)S(1)} all-to-all(bf16[32,4,384]{2,1,0:T(4,128)(2,1)S(1)} %join.1), channel_id=1, replica_groups={{26,27,24,25,30,31,28,29,18,19,16,17,22,23,20,21,10,11,8,9,14,15,12,13,..., dimensions={0} | all-to-all | bytes 196608 | tf_op jit(solution)/shard_map/all_to_all | solution.py:29
  32.8 0.5 %cycles.1 = bf16[16,4,128]{2,1,0:T(4,128)(2,1)S(1)} custom-call(bf16[32,4,384]{2,1,0:T(4,128)(2,1)S(1)} %all_to_all.15.received, bf16[128,128]{1,0:T(8,128)(2,1)S(1)} %get-tuple-element.20.pick), custom_call_target="tpu_custom_call" | custom-call | tf_op jit(solution)/shard_map/cycles/pallas_call | solution.py:298
  33.3 10.4 %all_to_all.16.grads = bf16[16,4,128]{2,1,0:T(4,128)(2,1)S(1)} all-to-all(bf16[16,4,128]{2,1,0:T(4,128)(2,1)S(1)} %cycles.1), channel_id=1, replica_groups={{288,256,352,320,416,384,480,448,32,0,96,64,160,128,224,192},{289,257,3..., dimensions={0} | all-to-all | bytes 32768 | tf_op jit(solution)/shard_map/all_to_all | solution.py:29
  43.7 0.8 %adjoint.1 = f32[3,4,1,256]{3,2,1,0:T(1,128)} custom-call(bf16[16,4,128]{2,1,0:T(4,128)(2,1)S(1)} %all_to_all.16.grads, bf16[512,128]{1,0:T(8,128)(2,1)S(1)} %get-tuple-element.21.legendre, f32[3,64,256]{2,1,0:T(8,128)S(1)} %get-tuple-element.22.mixed), custom_call_target="tpu_custom_call" | custom-call | tf_op jit(solution)/shard_map/adjoint/pallas_call | solution.py:305
  (1 shorter events, 0.0 us)
Async XLA Ops:
  1.8 16.0 %all-to-all-start = ((f32[16,4,128]{2,1,0:T(4,128)}), f32[16,4,128]{2,1,0:T(4,128)S(1)}, u32[]{:S(2)}, u32[]{:S(2)}) async-start(f32[16,4,128]{2,1,0:T(4,128)} %get-tuple-element.14), calls=%async_computation | async-start | bytes 65536 | tf_op jit(solution)/shard_map/all_to_all | solution.py:29
